TPU v7x, 512 devices: a whole 4x8x8 slice. The times are simulated.
512 devices in a mesh: dp: 64 (over y, z_hi, core), tensor: 8 (over z_lo, x).
Axes of the slice: x: 4, y: 8, z: 8 (z_hi: 4, z_lo: 2; z = z_hi * 2 + z_lo), core: 2. Of those that a mesh axis runs over, the one named last changes fastest.
Arguments:
- x_seq: bfloat16 [16384, 4096], P(('dp', 'tensor')), may hold values from -6 to 6
- weight: bfloat16 [4096, 2048], P(None, 'tensor'), may hold values from -0.09375 to 0.09375
- grad_out: bfloat16 [16384, 2048], P('dp', 'tensor'), may hold values from -6 to 6
- proj: bfloat16 [4096, 512], P('dp'), may hold values from -0.25 to 0.25
- moment1: float32 [512, 2048], P('dp', 'tensor'), may hold values from -6 to 6
- moment2: float32 [512, 2048], P('dp', 'tensor'), may hold values from 0.05 to 0.5
Outputs:
- values: bfloat16 [16384, 2048], P('dp', 'tensor')
- grad_in: bfloat16 [16384, 4096], P(('dp', 'tensor'))
- update: bfloat16 [4096, 2048], P(None, 'tensor')
- new_moment1: float32 [512, 2048], P('dp', 'tensor')
- new_moment2: float32 [512, 2048], P('dp', 'tensor')
All inputs are finite; a program needn't handle non-finite values.
Results may differ from a plain program's by a relative error of at most 0.017.
Values may be sent and summed in bfloat16 or wider, within the bound.
No kernel may reach another device: no remote copies, remote signals or barrier semaphores. Data moves between devices by JAX's collectives and lax.ppermute only.
A program may use at most 64 MiB of HBM per device.

v0:
```python
import math

import jax
import jax.numpy as jnp
from jax import lax
from jax.sharding import PartitionSpec as P


def per_device(x_seq, weight, grad_out, proj, moment1, moment2):
    full_x = lax.all_gather(x_seq, "tensor", axis=0, tiled=True)
    values = jnp.dot(full_x, weight, preferred_element_type=jnp.float32).astype(jnp.bfloat16)
    grad_in = lax.psum_scatter(
        lax.dot_general(
            grad_out, weight, (((1,), (1,)), ((), ())), preferred_element_type=jnp.float32
        ).astype(jnp.bfloat16),
        "tensor",
        scatter_dimension=0,
        tiled=True,
    )
    token_count = full_x.shape[0]
    inverse_root = 1.0 / math.sqrt(token_count)
    projected = jnp.dot(
        full_x, lax.all_gather(proj, "dp", axis=0, tiled=True), preferred_element_type=jnp.float32
    )
    local_coeff = lax.dot_general(
        projected,
        grad_out.astype(jnp.float32),
        (((0,), (0,)), ((), ())),
        precision=lax.Precision.HIGHEST,
    )
    coeff = lax.psum_scatter(local_coeff * inverse_root, "dp", scatter_dimension=0, tiled=True)
    new_moment1 = 0.9 * moment1 + 0.1 * coeff
    new_moment2 = 0.999 * moment2 + 0.001 * coeff * coeff
    step_dir = new_moment1 / (1.0 - 0.9**10) / (jnp.sqrt(new_moment2 / (1.0 - 0.999**10)) + 1e-08)
    full_step = lax.all_gather(step_dir, "dp", axis=0, tiled=True)
    local_update = jnp.dot(
        proj.astype(jnp.float32), full_step, precision=lax.Precision.HIGHEST
    ).astype(jnp.bfloat16)
    update = lax.all_gather(local_update, "dp", axis=0, tiled=True)
    return (values, grad_in, update, new_moment1, new_moment2)


def solution(mesh):
    placed = (
        P(("dp", "tensor"), None),
        P(None, "tensor"),
        P("dp", "tensor"),
        P("dp", None),
        P("dp", "tensor"),
        P("dp", "tensor"),
    )
    return jax.shard_map(
        per_device,
        mesh=mesh,
        in_specs=placed,
        out_specs=(
            P("dp", "tensor"),
            P(("dp", "tensor"), None),
            P(None, "tensor"),
            P("dp", "tensor"),
            P("dp", "tensor"),
        ),
        check_vma=False,
    )
```

profile of v0, /device:TPU:1, one launch (start us, length us, event | category | flops | bytes accessed | tf_op | source)
XLA Modules:
  0.0 518.5 jit_solution(12713560454885734671)
XLA Ops:
  7.2 0.0 copy-start
  7.2 0.0 all-gather.4.cloned.1.call-start
  7.2 0.7 all-gather.4.cloned.1.call-update
  7.9 0.0 all-gather.6.cloned.1.call-start
  8.0 0.7 all-gather.6.cloned.1.call-update
  8.7 0.0 reduce-scatter.5.cloned.1.call-start
  8.7 49.0 %all-gather.4.cloned.1.call-done = bf16[256,4096]{1,0:T(8,128)(2,1)} async-done(((bf16[32,4096]{1,0:T(8,128)(2,1)}), bf16[256,4096]{1,0:T(8,128)(2,1)}) %all-gather.4.cloned.1.call-update) | async-done | bytes 2097168 | tf_op jit(solution)/shard_map/all_gather | solution.py:10
  57.8 96.1 %all-gather.6.cloned.1.call-done = bf16[4096,512]{1,0:T(8,128)(2,1)} async-done(((bf16[64,512]{1,0:T(8,128)(2,1)}), bf16[4096,512]{1,0:T(8,128)(2,1)}) %all-gather.6.cloned.1.call-update) | async-done | bytes 4194320 | tf_op jit(solution)/shard_map/all_gather | solution.py:23
  153.9 4.1 fusion.3
  158.0 1.4 convolution_multiply_fusion
  159.4 0.0 reduce-scatter.5.cloned.1.call-update
  159.4 0.0 all-gather.8.cloned.1.call-start
  159.5 139.3 %reduce-scatter.5.cloned.1.call-done = f32[8,256]{1,0:T(8,128)} async-done(((f32[512,256]{1,0:T(8,128)}), f32[8,256]{1,0:T(8,128)}) %reduce-scatter.5.cloned.1.call-update) | async-done | bytes 8208 | tf_op jit(solution)/shard_map/reduce_scatter | solution.py:31
  298.8 1.3 add_divide_fusion
  300.1 85.8 %all_gather.14 = f32[512,256]{1,0:T(8,128)S(1)} all-gather(f32[8,256]{1,0:T(8,128)S(1)} %get-tuple-element.5), channel_id=1, replica_groups=mesh['dp'=64,'tensor'=8] {'dp'}, dimensions={0}, use_global_device_ids=true | all-gather | bytes 532480 | tf_op jit(solution)/shard_map/all_gather | solution.py:35
  385.9 0.9 fusion
  386.9 0.0 all-gather.8.cloned.1.call-update
  386.9 0.0 reduce-scatter.3.cloned.1.call-start
  387.0 2.1 convolution_convert_fusion
  389.0 0.0 reduce-scatter.3.cloned.1.call-update
  389.0 3.0 convolution_convert_fusion.1
  392.0 74.3 %all-gather.8.cloned.1.call-done = bf16[4096,256]{1,0:T(8,128)(2,1)} async-done(((bf16[64,256]{1,0:T(8,128)(2,1)}), bf16[4096,256]{1,0:T(8,128)(2,1)}) %all-gather.8.cloned.1.call-update) | async-done | bytes 2097168 | tf_op jit(solution)/shard_map/all_gather | solution.py:39
  466.3 42.7 %reduce-scatter.3.cloned.1.call-done = bf16[32,4096]{1,0:T(8,128)(2,1)} async-done(((bf16[256,4096]{1,0:T(8,128)(2,1)}), bf16[32,4096]{1,0:T(8,128)(2,1)}) %reduce-scatter.3.cloned.1.call-update) | async-done | bytes 262160 | tf_op jit(solution)/shard_map/reduce_scatter | solution.py:12
  509.0 3.0 copy.12
  (9 shorter events, 0.0 us)
Async XLA Ops:
  7.2 379.8 %copy-start = (bf16[4096,256]{1,0:T(8,128)(2,1)S(1)}, bf16[4096,256]{1,0:T(8,128)(2,1)}, u32[]{:S(2)}) copy-start(bf16[4096,256]{1,0:T(8,128)(2,1)} %param.7) | copy-start | bytes 6291460
  7.2 50.6 %all-gather.4.cloned.1.call-start = ((), (), s32[]{:S(2)}) async-start(), calls=%async_computation.2 | async-start | bytes 2359296 | tf_op jit(solution)/shard_map/all_gather | solution.py:10
  7.9 146.0 %all-gather.6.cloned.1.call-start = ((), (), s32[]{:S(2)}) async-start(), calls=%async_computation.4 | async-start | bytes 4259840 | tf_op jit(solution)/shard_map/all_gather | solution.py:23
  8.7 149.3 %copy-start.1 = (bf16[256,256]{1,0:T(8,128)(2,1)S(1)}, bf16[256,256]{1,0:T(8,128)(2,1)}, u32[]{:S(2)}) copy-start(bf16[256,256]{1,0:T(8,128)(2,1)} %param.8) | copy-start | bytes 393220
  8.7 290.1 %copy-start.3 = (f32[8,256]{1,0:T(8,128)S(1)}, f32[8,256]{1,0:T(8,128)}, u32[]{:S(2)}) copy-start(f32[8,256]{1,0:T(8,128)} %param.10) | copy-start | bytes 24580
  8.7 290.1 %copy-start.4 = (f32[8,256]{1,0:T(8,128)S(1)}, f32[8,256]{1,0:T(8,128)}, u32[]{:S(2)}) copy-start(f32[8,256]{1,0:T(8,128)} %param.11) | copy-start | bytes 24580
  8.7 290.1 %reduce-scatter.5.cloned.1.call-start = ((), (), s32[]{:S(2)}) async-start(), calls=%async_computation.5 | async-start | bytes 532480 | tf_op jit(solution)/shard_map/reduce_scatter | solution.py:31
  158.0 228.0 %copy-start.2 = (bf16[64,512]{1,0:T(8,128)(2,1)S(1)}, bf16[64,512]{1,0:T(8,128)(2,1)}, u32[]{:S(2)}) copy-start(bf16[64,512]{1,0:T(8,128)(2,1)} %param.9) | copy-start | bytes 196612
  159.4 306.8 %all-gather.8.cloned.1.call-start = ((), (), s32[]{:S(2)}) async-start(), calls=%async_computation.6 | async-start | bytes 2129920 | tf_op jit(solution)/shard_map/all_gather | solution.py:39
  386.9 122.1 %reduce-scatter.3.cloned.1.call-start = ((), (), s32[]{:S(2)}) async-start(), calls=%async_computation.3 | async-start | bytes 2359296 | tf_op jit(solution)/shard_map/reduce_scatter | solution.py:12
Sparse Core Ops, SparseCore 0:
  10.1 47.6 all-gather.3
  61.1 92.7 all-gather.5
  159.5 139.2 reduce-scatter.4
  387.0 79.2 all-gather.7
  469.5 39.4 reduce-scatter.2
where the time goes:
time: 523 us; the launch traced here: 519 us
  waiting for transfers between devices  403 us (77%)
  blocking collectives  85.8 us (16%)
  between operations  13.8 us (3%)
  matrix products  11.4 us (2%)
    reduce_scatter x1, waiting for transfers between devices, per_device(): lax.psum_scatter(local_coeff * inverse_root, 'dp', scatter_dimension=0, t...  139 us
    all_gather x1, waiting for transfers between devices, per_device(): lax.all_gather(proj, 'dp', axis=0, tiled=True)  96.1 us
    all_gather x1, blocking collectives, per_device(): full_step = lax.all_gather(step_dir, 'dp', axis=0, tiled=True)  85.8 us
    all_gather x1, waiting for transfers between devices, per_device(): update = lax.all_gather(local_update, 'dp', axis=0, tiled=True)  74.3 us
    all_gather x1, waiting for transfers between devices, per_device(): full_x = lax.all_gather(x_seq, 'tensor', axis=0, tiled=True)  49 us
    reduce_scatter x1, waiting for transfers between devices, per_device(): lax.psum_scatter(lax.dot_general(grad_out, weight, (((1,), (1,)), ((), ()...  42.7 us
  transfers between devices with their start and end apart: 5, of which 5 were waited for; matrix products, arithmetic and copies ran while one was open for 1% of the time, Pallas kernels for 0%

commit v1 on v0

v1 whole, which is shorter than its diff:
```python
import math

import jax
import jax.numpy as jnp
from jax import lax
from jax.sharding import Mesh
from jax.sharding import PartitionSpec as P

AXES = ("y", "zh", "c", "zl", "x")
DP = ("y", "zh", "c")
RING = ("y", "zh")
TENSOR = ("zl", "x")
SWAP = [(0, 1), (1, 0)]


def copies_to(value, axes, count):
    copies = jnp.broadcast_to(value[None], (count, *value.shape))
    return lax.all_to_all(copies, axes, 0, 0, tiled=True)


def split(value):
    high = value.astype(jnp.bfloat16)
    return high, (value - high.astype(jnp.float32)).astype(jnp.bfloat16)


def per_device(x_seq, weight, grad_out, proj, moment1, moment2):
    first = lax.axis_index("c") == 0
    tokens, heads = grad_out.shape
    rows, rank = proj.shape
    count = 32

    def own_other(a, b):
        return jnp.where(first, a, b), jnp.where(first, b, a)

    proj_z = copies_to(proj, "zh", 4)
    x_seq, proj_z = lax.optimization_barrier((x_seq, proj_z))
    proj_own = lax.all_gather(proj_z.reshape(4 * rows, rank), "y", axis=0, tiled=True)

    x_split = x_seq.reshape(x_seq.shape[0], count, 2, rows)
    x_ordered = jnp.concatenate(own_other(x_split[:, :, 0], x_split[:, :, 1]), axis=1)
    full_x = copies_to(x_ordered.reshape(x_seq.shape), TENSOR, 8).reshape(tokens, -1)
    w_split = weight.reshape(count, 2, rows, heads)
    w_ordered = jnp.concatenate(own_other(w_split[:, 0], w_split[:, 1]), axis=0).reshape(weight.shape)
    values = jnp.dot(full_x, w_ordered, preferred_element_type=jnp.float32).astype(jnp.bfloat16)

    proj_other = lax.ppermute(proj_own, "c", SWAP)
    half = count * rows
    projected = jnp.dot(full_x[:, :half], proj_own, preferred_element_type=jnp.float32)
    projected += jnp.dot(full_x[:, half:], proj_other, preferred_element_type=jnp.float32)

    dims = (((0,), (0,)), ((), ()))
    local = sum(
        lax.dot_general(part, grad_out, dims, preferred_element_type=jnp.float32) for part in split(projected)
    )
    local = (local * (1.0 / math.sqrt(tokens))).reshape(count, 2, rank // 64, heads)
    mine, theirs = own_other(local[:, 0], local[:, 1])
    chip = mine + lax.ppermute(theirs, "c", SWAP)
    coeff = jnp.sum(lax.all_to_all(chip, RING, 0, 0, tiled=True), axis=0)

    new_moment1 = 0.9 * moment1 + 0.1 * coeff
    new_moment2 = 0.999 * moment2 + 0.001 * coeff * coeff
    step_dir = new_moment1 / (1.0 - 0.9**10) / (jnp.sqrt(new_moment2 / (1.0 - 0.999**10)) + 1e-08)

    step_own = copies_to(step_dir, RING, count)
    step = jnp.stack(own_other(step_own, lax.ppermute(step_own, "c", SWAP)), axis=1).reshape(rank, heads)
    steps = split(step)

    def update_rows(basis):
        return sum(jnp.dot(basis, part, preferred_element_type=jnp.float32) for part in steps).astype(jnp.bfloat16)

    pair = own_other(update_rows(proj_own), update_rows(proj_other))
    update = jnp.stack([u.reshape(count, rows, heads) for u in pair], axis=1).reshape(weight.shape)

    grad_out, _ = lax.optimization_barrier((grad_out, proj_other))
    grad_in = lax.psum_scatter(
        lax.dot_general(grad_out, weight, (((1,), (1,)), ((), ())), preferred_element_type=jnp.float32).astype(
            jnp.bfloat16
        ),
        TENSOR,
        scatter_dimension=0,
        tiled=True,
    )
    return (values, grad_in, update, new_moment1, new_moment2)


def solution(mesh):
    fine = Mesh(mesh.devices.reshape(8, 4, 2, 2, 4), AXES)
    placed = (P(AXES, None), P(None, TENSOR), P(DP, TENSOR), P(DP, None), P(DP, TENSOR), P(DP, TENSOR))
    return jax.shard_map(
        per_device,
        mesh=fine,
        in_specs=placed,
        out_specs=(P(DP, TENSOR), P(AXES, None), P(None, TENSOR), P(DP, TENSOR), P(DP, TENSOR)),
        check_vma=False,
    )
```

time: 523 us -> 150 us (0.29)
  waiting for transfers between devices: 403 us -> 41.5 us
  blocking collectives: 85.8 us -> 42.6 us
  starting transfers between devices: 0.2 us -> 25 us
  local copies, waits for them, and re-layouts: 3.07 us -> 10.3 us
    all_gather x3 -> x1, waiting for transfers between devices: 219 us -> 28.5 us  [per_device(): lax.all_gather(proj_z.reshape(4 * rows, rank), 'y', axis=0, tiled=True)]
    reduce_scatter x1 -> x0, waiting for transfers between devices: 139 us -> none  [per_device(): lax.psum_scatter(local_coeff * inverse_root, 'dp', scatter_dimension=0, t...]
    all_gather x1 -> x0, blocking collectives: 85.8 us -> none  [per_device(): full_step = lax.all_gather(step_dir, 'dp', axis=0, tiled=True)]
    reduce_scatter x1, waiting for transfers between devices: 42.7 us -> 0.01 us  [per_device(): lax.psum_scatter(lax.dot_general(grad_out, weight, (((1,), (1,)), ((), ()...]
    all_to_all x0 -> x2, blocking collectives: none -> 42.6 us  [the longest x1 23.1 us: per_device(): coeff = jnp.sum(lax.all_to_all(chip, RING, 0, 0, tiled=True), axis=0)]
    ppermute x0 -> x3, starting transfers between devices: none -> 12.9 us  [the longest x1 6.1 us: per_device(): proj_other = lax.ppermute(proj_own, 'c', SWAP)]
    all_to_all x0 -> x2, starting transfers between devices: none -> 11.9 us  [copies_to(): return lax.all_to_all(copies, axes, 0, 0, tiled=True)]
    all_to_all x0 -> x2, waiting for transfers between devices: none -> 11.7 us  [copies_to(): return lax.all_to_all(copies, axes, 0, 0, tiled=True)]
  transfers between devices with their start and end apart: 5 -> 7, of which waited for: 5 -> 3; matrix products, arithmetic and copies ran while one was open for 1% -> 13% of each run, Pallas kernels for 0% -> 0%
where the time goes in v1:
time: 150 us
  blocking collectives  42.6 us (28%)
  waiting for transfers between devices  41.5 us (28%)
  starting transfers between devices  25 us (17%)
  between operations  14.3 us (10%)
  matrix products  13 us (9%)
  local copies, waits for them, and re-layouts  10.3 us (7%)
  other arithmetic  2.81 us (2%)
    all_gather x1, waiting for transfers between devices, per_device(): lax.all_gather(proj_z.reshape(4 * rows, rank), 'y', axis=0, tiled=True)  28.5 us
    all_to_all x1, blocking collectives, per_device(): coeff = jnp.sum(lax.all_to_all(chip, RING, 0, 0, tiled=True), axis=0)  23.1 us
    all_to_all x1, blocking collectives, copies_to(): return lax.all_to_all(copies, axes, 0, 0, tiled=True)  19.5 us
    all_to_all x2, starting transfers between devices, copies_to(): return lax.all_to_all(copies, axes, 0, 0, tiled=True)  11.9 us
    all_to_all x2, waiting for transfers between devices, copies_to(): return lax.all_to_all(copies, axes, 0, 0, tiled=True)  11.7 us
    ppermute x1, starting transfers between devices, per_device(): proj_other = lax.ppermute(proj_own, 'c', SWAP)  6.1 us
    ppermute x1, starting transfers between devices, per_device(): lax.ppermute(step_own, 'c', SWAP)  4.43 us
    unnamed x15, local copies, waits for them, and re-layouts  3.77 us
  transfers between devices with their start and end apart: 7, of which 3 were waited for; matrix products, arithmetic and copies ran while one was open for 13% of the time, Pallas kernels for 0%

profile of v1, /device:TPU:1, one launch (start us, length us, event | category | flops | bytes accessed | tf_op | source)
XLA Modules:
  0.0 149.5 jit_solution(4842393882473679241)
XLA Ops:
  7.2 0.9 broadcast_in_dim.8
  8.1 19.5 %all_to_all.20 = bf16[4,64,512]{2,1,0:T(8,128)(2,1)} all-to-all(bf16[4,64,512]{2,1,0:T(8,128)(2,1)S(1)} %broadcast_in_dim.8), channel_id=1, replica_groups=mesh['y'=8,'zh'=4,'c'=2,'zl'=2,'x'=4] {'zh'}, dimensions={0} | all-to-all | bytes 524288 | tf_op jit(solution)/shard_map/all_to_all | solution.py:18
  27.6 1.5 reshape.49
  29.1 1.2 broadcast_select_fusion.3
  31.0 1.6 %broadcast_in_dim.10 = bf16[8,32,4096]{2,1,0:T(8,128)(2,1)} broadcast(bf16[32,4096]{1,0:T(8,128)(2,1)S(1)} %broadcast_in_dim.9), dimensions={1,2} | broadcast | bytes 2359296 | tf_op jit(solution)/shard_map/broadcast_in_dim | solution.py:17
  32.6 6.4 %all-to-all-start.1 = ((bf16[8,32,4096]{2,1,0:T(8,128)(2,1)}), bf16[8,32,4096]{2,1,0:T(8,128)(2,1)}, u32[]{:S(2)}, u32[]{:S(2)}) async-start(bf16[8,32,4096]{2,1,0:T(8,128)(2,1)} %broadcast_in_dim.10), calls=%async_computation.1 | async-start | bytes 4194304 | tf_op jit(solution)/shard_map/all_to_all | solution.py:18
  39.0 28.5 %all-gather.2.cloned.1.call-done = bf16[2048,512]{1,0:T(8,128)(2,1)} async-done(((bf16[256,512]{1,0:T(8,128)(2,1)}), bf16[2048,512]{1,0:T(8,128)(2,1)}) %all-gather.2.cloned.1.call-update) | async-done | bytes 2097168 | tf_op jit(solution)/shard_map/all_gather | solution.py:37
  67.5 6.1 %collective-permute-start = (bf16[2048,512]{1,0:T(8,128)(2,1)}, bf16[2048,512]{1,0:T(8,128)(2,1)S(1)}, u32[]{:S(2)}, u32[]{:S(2)}) collective-permute-start(bf16[2048,512]{1,0:T(8,128)(2,1)} %all-gather.2.cloned.1.call-done), channel_id=1, source_target_pairs={{0,8},{8,0},{1,9},{9,1},{2,10},{10,2},{3,11},{11,3},{4,12},{12,4},... | collective-permute-start | bytes 6291464 | tf_op jit(solution)/shard_map/ppermute | solution.py:46
  73.6 2.6 %fusion.5 = f32[256,512]{1,0:T(8,128)S(1)} fusion(bf16[2048,512]{1,0:T(8,128)(2,1)} %all-gather.2.cloned.1.call-done, bf16[256,4096]{1,0:T(8,128)(2,1)} %bitcast), kind=kOutput, calls=%fused_computation.14 | convolution fusion | flops 536870912 | bytes 3670016 | tf_op jit(solution)/shard_map/dot_general | solution.py:48
  76.3 1.3 collective-permute-done
  77.6 1.3 copy-done.3
  78.9 1.9 %convolution_add_fusion.2 = f32[256,512]{1,0:T(8,128)S(1)} fusion(f32[256,512]{1,0:T(8,128)S(1)} %fusion.5, bf16[2048,512]{1,0:T(8,128)(2,1)S(1)} %collective-permute-done, bf16[256,4096]{1,0:T(8,128)(2,1)} %bitcast), kind=kOutput, calls=%fused_computation.8 | convolution fusion | flops 537001984 | bytes 4194304 | tf_op jit(solution)/shard_map/dot_general | solution.py:49
  81.5 2.4 %collective-permute-start.1 = (f32[32,8,256]{2,1,0:T(8,128)S(1)}, f32[32,8,256]{2,1,0:T(8,128)S(1)}, u32[]{:S(2)}, u32[]{:S(2)}) collective-permute-start(f32[32,8,256]{2,1,0:T(8,128)S(1)} %select_bitcast_fusion.2), channel_id=1, source_target_pairs={{0,8},{8,0},{1,9},{9,1},{2,10},{10,2},{3,11},{11,3},{4,12},{12,4},... | collective-permute-start | bytes 786440 | tf_op jit(solution)/shard_map/ppermute | solution.py:57
  83.9 2.1 %convolution_convert_fusion = bf16[256,4096]{1,0:T(8,128)(2,1)} fusion(bf16[256,256]{1,0:T(8,128)(2,1)S(1)} %copy-done, bf16[4096,256]{1,0:T(8,128)(2,1)S(1)} %copy-done.1), kind=kOutput, calls=%fused_computation | convolution fusion | flops 537919488 | bytes 4325376 | tf_op jit(solution)/shard_map/dot_general | solution.py:76
  86.1 23.1 %all_to_all.21 = f32[32,8,256]{2,1,0:T(8,128)S(1)} all-to-all(f32[32,8,256]{2,1,0:T(8,128)S(1)} %fusion.10), channel_id=1, replica_groups=mesh['y'=8,'zh'=4,'c'=2,'zl'=2,'x'=4] {'y','zh'}, dimensions={0} | all-to-all | bytes 524288 | tf_op jit(solution)/shard_map/all_to_all | solution.py:58
  109.9 0.7 broadcast_in_dim.22
  110.6 5.6 %all-to-all-start.3 = ((f32[32,8,256]{2,1,0:T(8,128)}), f32[32,8,256]{2,1,0:T(8,128)S(1)}, u32[]{:S(2)}, u32[]{:S(2)}) async-start(f32[32,8,256]{2,1,0:T(8,128)} %broadcast_in_dim.22), calls=%async_computation.4 | async-start | bytes 524288 | tf_op jit(solution)/shard_map/all_to_all | solution.py:18
  116.6 11.6 %all-to-all-done.3 = f32[32,8,256]{2,1,0:T(8,128)S(1)} async-done(((f32[32,8,256]{2,1,0:T(8,128)}), f32[32,8,256]{2,1,0:T(8,128)S(1)}, u32[]{:S(2)}, u32[]{:S(2)}) %all-to-all-start.3) | async-done | bytes 262176 | tf_op jit(solution)/shard_map/all_to_all | solution.py:18
  128.3 4.4 %collective-permute-start.2 = (f32[32,8,256]{2,1,0:T(8,128)S(1)}, f32[32,8,256]{2,1,0:T(8,128)S(1)}, u32[]{:S(2)}, u32[]{:S(2)}) collective-permute-start(f32[32,8,256]{2,1,0:T(8,128)S(1)} %all-to-all-done.3), channel_id=1, source_target_pairs={{0,8},{8,0},{1,9},{9,1},{2,10},{10,2},{3,11},{11,3},{4,12},{12,4},... | collective-permute-start | bytes 786440 | tf_op jit(solution)/shard_map/ppermute | solution.py:65
  132.7 3.0 %convolution_convert_fusion.1 = bf16[256,256]{1,0:T(8,128)(2,1)} fusion(bf16[256,4096]{1,0:T(8,128)(2,1)} %bitcast, bf16[4096,256]{1,0:T(8,128)(2,1)S(1)} %bitcast.81), kind=kOutput, calls=%fused_computation.11 | convolution fusion | flops 536936448 | bytes 4325376 | tf_op jit(solution)/shard_map/dot_general | solution.py:44
  135.8 1.5 copy-done.2
  138.0 0.9 copy-done.4
  139.6 0.7 fusion
  141.2 1.5 copy.53
  (38 shorter events, 4.9 us)
Async XLA Ops:
  7.2 73.7 %copy-start = (bf16[256,256]{1,0:T(8,128)(2,1)S(1)}, bf16[256,256]{1,0:T(8,128)(2,1)}, u32[]{:S(2)}) copy-start(bf16[256,256]{1,0:T(8,128)(2,1)} %param.8) | copy-start | bytes 393220
  7.2 60.3 %all-gather.2.cloned.1.call-start = ((), (), s32[]{:S(2)}) async-start(), calls=%async_computation.5 | async-start | bytes 2359296 | tf_op jit(solution)/shard_map/all_gather | solution.py:37
  32.6 41.0 %all-to-all-start.1 = ((bf16[8,32,4096]{2,1,0:T(8,128)(2,1)}), bf16[8,32,4096]{2,1,0:T(8,128)(2,1)}, u32[]{:S(2)}, u32[]{:S(2)}) async-start(bf16[8,32,4096]{2,1,0:T(8,128)(2,1)} %broadcast_in_dim.10), calls=%async_computation.1 | async-start | bytes 4194304 | tf_op jit(solution)/shard_map/all_to_all | solution.py:18
  39.0 103.7 %reduce-scatter.2.cloned.1.call-start = ((), (), s32[]{:S(2)}) async-start(), calls=%async_computation.6 | async-start | bytes 2359296 | tf_op jit(solution)/shard_map/reduce_scatter | solution.py:75
  67.5 10.1 %collective-permute-start = (bf16[2048,512]{1,0:T(8,128)(2,1)}, bf16[2048,512]{1,0:T(8,128)(2,1)S(1)}, u32[]{:S(2)}, u32[]{:S(2)}) collective-permute-start(bf16[2048,512]{1,0:T(8,128)(2,1)} %all-gather.2.cloned.1.call-done), channel_id=1, source_target_pairs={{0,8},{8,0},{1,9},{9,1},{2,10},{10,2},{3,11},{11,3},{4,12},{12,4},... | collective-permute-start | bytes 6291464 | tf_op jit(solution)/shard_map/ppermute | solution.py:46
  77.6 1.3 copy-start.3
  80.9 3.0 %copy-start.1 = (bf16[4096,256]{1,0:T(8,128)(2,1)S(1)}, bf16[4096,256]{1,0:T(8,128)(2,1)}, u32[]{:S(2)}) copy-start(bf16[4096,256]{1,0:T(8,128)(2,1)} %param.7) | copy-start | bytes 6291460
  81.5 4.6 %collective-permute-start.1 = (f32[32,8,256]{2,1,0:T(8,128)S(1)}, f32[32,8,256]{2,1,0:T(8,128)S(1)}, u32[]{:S(2)}, u32[]{:S(2)}) collective-permute-start(f32[32,8,256]{2,1,0:T(8,128)S(1)} %select_bitcast_fusion.2), channel_id=1, source_target_pairs={{0,8},{8,0},{1,9},{9,1},{2,10},{10,2},{3,11},{11,3},{4,12},{12,4},... | collective-permute-start | bytes 786440 | tf_op jit(solution)/shard_map/ppermute | solution.py:57
  86.0 23.3 %copy-start.5 = (f32[8,256]{1,0:T(8,128)S(1)}, f32[8,256]{1,0:T(8,128)}, u32[]{:S(2)}) copy-start(f32[8,256]{1,0:T(8,128)} %param.10) | copy-start | bytes 24580
  86.0 23.3 %copy-start.6 = (f32[8,256]{1,0:T(8,128)S(1)}, f32[8,256]{1,0:T(8,128)}, u32[]{:S(2)}) copy-start(f32[8,256]{1,0:T(8,128)} %param.11) | copy-start | bytes 24580
  110.6 17.6 %all-to-all-start.3 = ((f32[32,8,256]{2,1,0:T(8,128)}), f32[32,8,256]{2,1,0:T(8,128)S(1)}, u32[]{:S(2)}, u32[]{:S(2)}) async-start(f32[32,8,256]{2,1,0:T(8,128)} %broadcast_in_dim.22), calls=%async_computation.4 | async-start | bytes 524288 | tf_op jit(solution)/shard_map/all_to_all | solution.py:18
  128.3 7.4 %collective-permute-start.2 = (f32[32,8,256]{2,1,0:T(8,128)S(1)}, f32[32,8,256]{2,1,0:T(8,128)S(1)}, u32[]{:S(2)}, u32[]{:S(2)}) collective-permute-start(f32[32,8,256]{2,1,0:T(8,128)S(1)} %all-to-all-done.3), channel_id=1, source_target_pairs={{0,8},{8,0},{1,9},{9,1},{2,10},{10,2},{3,11},{11,3},{4,12},{12,4},... | collective-permute-start | bytes 786440 | tf_op jit(solution)/shard_map/ppermute | solution.py:65
  135.7 1.6 %copy-start.2 = (bf16[2048,512]{1,0:T(8,128)(2,1)S(1)}, bf16[2048,512]{1,0:T(8,128)(2,1)}, u32[]{:S(2)}) copy-start(bf16[2048,512]{1,0:T(8,128)(2,1)} %all-gather.2.cloned.1.call-done) | copy-start | bytes 6291460
  137.3 1.6 %copy-start.4 = (bf16[2048,512]{1,0:T(8,128)(2,1)S(1)}, bf16[2048,512]{1,0:T(8,128)(2,1)}, u32[]{:S(2)}) copy-start(bf16[2048,512]{1,0:T(8,128)(2,1)} %copy-done.3) | copy-start | bytes 6291460
Sparse Core Ops, SparseCore 0:
  27.7 39.7 all-gather.1
  86.2 49.8 reduce-scatter.1

commit v2 on v1

v2 whole, which is shorter than its diff:
```python
import math

import jax
import jax.numpy as jnp
from jax import lax
from jax.experimental import pallas as pl
from jax.experimental.pallas import tpu as pltpu
from jax.sharding import Mesh
from jax.sharding import PartitionSpec as P

AXES = ("y", "zh", "c", "zl", "x")
DP = ("y", "zh", "c")
RING = ("y", "zh")
TENSOR = ("zl", "x")
SWAP = [(0, 1), (1, 0)]
bf16, f32 = jnp.bfloat16, jnp.float32


def copies_to(value, axes, count):
    copies = jnp.broadcast_to(value[None], (count, *value.shape))
    return lax.all_to_all(copies, axes, 0, 0, tiled=True)


def update_rows(cores, basis_own, basis_other, step, rows):
    parts, half, width = basis_own.shape
    heads = step.shape[1]
    blocks = 4

    def kernel(core_ref, own_ref, other_ref, step_ref, out_ref):
        for ref, place in ((own_ref, core_ref[0]), (other_ref, core_ref[1])):
            for i in range(half // (blocks * rows)):
                lines = slice(i * blocks * rows, (i + 1) * blocks * rows)
                line = jnp.concatenate([ref[k, lines, :] for k in range(parts)], axis=1)
                block = jnp.dot(line, step_ref[...], preferred_element_type=f32).astype(bf16)
                out_ref[i * blocks : (i + 1) * blocks, pl.ds(place, 1)] = block.reshape(blocks, 1, rows, heads)

    vmem = pl.BlockSpec(memory_space=pltpu.VMEM)
    out = pl.pallas_call(
        kernel,
        out_shape=jax.ShapeDtypeStruct((half // rows, 2, rows, heads), bf16),
        in_specs=[pl.BlockSpec(memory_space=pltpu.SMEM), vmem, vmem, vmem],
        out_specs=vmem,
        compiler_params=pltpu.CompilerParams(vmem_limit_bytes=24 * 2**20),
        cost_estimate=pl.CostEstimate(
            flops=4 * half * parts * width * heads,
            bytes_accessed=4 * half * (parts * width + heads),
            transcendentals=0,
        ),
    )(cores, basis_own, basis_other, step)
    return out.reshape(2 * half, heads)


def per_device(x_seq, weight, grad_out, proj, moment1, moment2):
    core = lax.axis_index("c")
    first = core == 0
    tokens, heads = grad_out.shape
    rows, rank = proj.shape
    features = weight.shape[0]
    own_tokens = x_seq.shape[0]
    count = 32
    half = count * rows
    dims = (((0,), (0,)), ((), ()))

    def ordered(own, other):
        return [jnp.where(first, own, other), jnp.where(first, other, own)]

    def swap(value):
        return lax.ppermute(value, "c", SWAP)

    proj_z = copies_to(proj, "zh", 4)
    x_seq, grad_out, moment1, proj_z = lax.optimization_barrier((x_seq, grad_out, moment1, proj_z))
    proj_own = lax.all_gather(proj_z.reshape(4 * rows, rank), "y", axis=0, tiled=True)

    x_split = x_seq.reshape(own_tokens, count, 2, rows)
    x_own, x_other = (v.reshape(own_tokens, half) for v in ordered(x_split[:, :, 0], x_split[:, :, 1]))
    both_x = copies_to(jnp.stack([x_own, swap(x_other)]), TENSOR, 8).reshape(2 * tokens, half)

    terms = lax.dot_general(grad_out, weight, (((1,), (1,)), ((), ())), preferred_element_type=f32).astype(bf16)
    grads = [g.reshape(8, own_tokens, heads) for g in (grad_out, swap(grad_out))]
    both_grads = jnp.stack(grads, axis=1).reshape(2 * tokens, heads)
    moments = jnp.stack([moment1, moment2])
    moments = jnp.stack(ordered(moments, swap(moments)), axis=1).reshape(2, 2 * moment1.shape[0], heads)
    proj_own, terms, both_grads, moments = lax.optimization_barrier((proj_own, terms, both_grads, moments))
    grad_in = lax.psum_scatter(terms, TENSOR, scatter_dimension=0, tiled=True)

    projected = jnp.dot(both_x, proj_own, preferred_element_type=f32).astype(bf16)
    projected = lax.optimization_barrier(projected)
    local = lax.dot_general(projected, both_grads, dims, preferred_element_type=f32)
    local = (local * (1.0 / math.sqrt(tokens))).astype(bf16).reshape(count, -1, heads)
    chip = jnp.sum(lax.all_to_all(local, RING, 0, 0, tiled=True).astype(f32), axis=0)
    coeff = chip + swap(chip)
    both1 = 0.9 * moments[0] + 0.1 * coeff
    both2 = 0.999 * moments[1] + 0.001 * coeff * coeff
    step_dir = both1 / (1.0 - 0.9**10) / (jnp.sqrt(both2 / (1.0 - 0.999**10)) + 1e-08)
    new_moment1, new_moment2 = (jnp.where(first, m[:8], m[8:]) for m in (both1, both2))

    proj_other = swap(proj_own)
    w_split = weight.reshape(count, 2, rows, heads)
    w_own = jnp.where(first, w_split[:, 0], w_split[:, 1]).reshape(half, heads)
    parts = jnp.dot(both_x, w_own, preferred_element_type=f32).reshape(8, 2, own_tokens, heads)
    values = (parts[:, 0] + swap(parts[:, 1])).astype(bf16).reshape(tokens, heads)

    step = copies_to(step_dir.astype(bf16), RING, count).reshape(rank, heads)
    update = update_rows(jnp.stack([core, 1 - core]), proj_own[None], proj_other[None], step, rows)
    return (values, grad_in, update, new_moment1, new_moment2)


def solution(mesh):
    fine = Mesh(mesh.devices.reshape(8, 4, 2, 2, 4), AXES)
    placed = (P(AXES, None), P(None, TENSOR), P(DP, TENSOR), P(DP, None), P(DP, TENSOR), P(DP, TENSOR))
    return jax.shard_map(
        per_device,
        mesh=fine,
        in_specs=placed,
        out_specs=(P(DP, TENSOR), P(AXES, None), P(None, TENSOR), P(DP, TENSOR), P(DP, TENSOR)),
        check_vma=False,
    )
```

time: 150 us -> 139 us (0.927)
  blocking collectives: 42.6 us -> 19.5 us
  starting transfers between devices: 25 us -> 41.4 us
  matrix products: 13 us -> 8.27 us
  Pallas kernels: 0 us -> 4.18 us
  waiting for transfers between devices: 41.5 us -> 38.4 us
  local copies, waits for them, and re-layouts: 10.3 us -> 7.93 us
    all_to_all x1 -> x0, blocking collectives: 23.1 us -> none  [per_device(): coeff = jnp.sum(lax.all_to_all(chip, RING, 0, 0, tiled=True), axis=0)]
    all_gather x1, waiting for transfers between devices: 28.5 us -> 17.2 us  [per_device(): lax.all_gather(proj_z.reshape(4 * rows, rank), 'y', axis=0, tiled=True)]
    all_to_all x0 -> x1, starting transfers between devices: none -> 10.4 us  [per_device(): lax.all_to_all(local, RING, 0, 0, tiled=True).astype(f32)]
    all_to_all x0 -> x1, waiting for transfers between devices: none -> 9.21 us  [per_device(): lax.all_to_all(local, RING, 0, 0, tiled=True).astype(f32)]
    ppermute x3 -> x6, starting transfers between devices: 12.9 us -> 21.7 us  [swap(): return lax.ppermute(value, 'c', SWAP)]
    dot_general x9 -> x3, matrix products: 10.9 us -> 6.2 us  [the longest x1 2.83 us: per_device(): jnp.dot(both_x, proj_own, preferred_element_type=f32).astype(bf16)]
    pallas_call x0 -> x1, Pallas kernels: none -> 4.18 us  [update_rows(): pl.pallas_call(kernel, out_shape=jax.ShapeDtypeStruct((half // rows, 2, r...]
    all_to_all x2, starting transfers between devices: 11.9 us -> 9.26 us  [copies_to(): return lax.all_to_all(copies, axes, 0, 0, tiled=True)]
  transfers between devices with their start and end apart: 7 -> 11, of which waited for: 3 -> 4; matrix products, arithmetic and copies ran while one was open for 13% -> 12% of each run, Pallas kernels for 0% -> 3%
where the time goes in v2:
time: 139 us; the launch traced here: 137 us
  starting transfers between devices  41.4 us (30%)
  waiting for transfers between devices  38.4 us (28%)
  blocking collectives  19.5 us (14%)
  between operations  14.3 us (10%)
  matrix products  8.27 us (6%)
  local copies, waits for them, and re-layouts  7.93 us (6%)
  Pallas kernels  4.18 us (3%)
  other arithmetic  3.25 us (2%)
    ppermute x6, starting transfers between devices, swap(): return lax.ppermute(value, 'c', SWAP)  21.7 us
    all_to_all x1, blocking collectives, copies_to(): return lax.all_to_all(copies, axes, 0, 0, tiled=True)  19.5 us
    all_gather x1, waiting for transfers between devices, per_device(): lax.all_gather(proj_z.reshape(4 * rows, rank), 'y', axis=0, tiled=True)  17.2 us
    all_to_all x2, waiting for transfers between devices, copies_to(): return lax.all_to_all(copies, axes, 0, 0, tiled=True)  11.3 us
    all_to_all x1, starting transfers between devices, per_device(): lax.all_to_all(local, RING, 0, 0, tiled=True).astype(f32)  10.4 us
    all_to_all x2, starting transfers between devices, copies_to(): return lax.all_to_all(copies, axes, 0, 0, tiled=True)  9.26 us
    all_to_all x1, waiting for transfers between devices, per_device(): lax.all_to_all(local, RING, 0, 0, tiled=True).astype(f32)  9.21 us
    pallas_call x1, Pallas kernels, update_rows(): pl.pallas_call(kernel, out_shape=jax.ShapeDtypeStruct((half // rows, 2, r...  4.18 us
  transfers between devices with their start and end apart: 11, of which 4 were waited for; matrix products, arithmetic and copies ran while one was open for 12% of the time, Pallas kernels for 3%

profile of v2, /device:TPU:1, one launch (start us, length us, event | category | flops | bytes accessed | tf_op | source)
XLA Modules:
  0.0 137.2 jit_solution(17259796266248794307)
XLA Ops:
  7.2 0.9 broadcast_in_dim.10
  8.1 19.5 %all_to_all.20 = bf16[4,64,512]{2,1,0:T(8,128)(2,1)} all-to-all(bf16[4,64,512]{2,1,0:T(8,128)(2,1)S(1)} %broadcast_in_dim.10), channel_id=1, replica_groups=mesh['y'=8,'zh'=4,'c'=2,'zl'=2,'x'=4] {'zh'}, dimensions={0} | all-to-all | bytes 524288 | tf_op jit(solution)/shard_map/all_to_all | solution.py:21
  27.6 1.5 %reshape.78 = bf16[32,32,2,64]{3,2,1,0:T(2,128)(2,1)S(1)} reshape(bf16[32,4096]{1,0:T(8,128)(2,1)} %param.6) | data formatting | bytes 524288 | tf_op jit(solution)/shard_map/reshape | solution.py:74
  29.1 1.2 fusion.5
  30.6 5.6 %collective-permute-start = (bf16[32,2048]{1,0:T(8,128)(2,1)S(1)}, bf16[32,2048]{1,0:T(8,128)(2,1)S(1)}, u32[]{:S(2)}, u32[]{:S(2)}) collective-permute-start(bf16[32,2048]{1,0:T(8,128)(2,1)S(1)} %select_n.66), channel_id=1, source_target_pairs={{0,8},{8,0},{1,9},{9,1},{2,10},{10,2},{3,11},{11,3},{4,12},{12,4},... | collective-permute-start | bytes 393224 | tf_op jit(solution)/shard_map/ppermute | solution.py:68
  37.2 1.6 %broadcast_in_dim.11 = bf16[8,2,32,2048]{3,2,1,0:T(8,128)(2,1)} broadcast(bf16[2,32,2048]{2,1,0:T(8,128)(2,1)S(1)} %pad_maximum_fusion), dimensions={1,2,3} | broadcast | bytes 2359296 | tf_op jit(solution)/shard_map/broadcast_in_dim | solution.py:20
  38.8 4.7 %all-to-all-start.1 = ((bf16[8,2,32,2048]{3,2,1,0:T(8,128)(2,1)}), bf16[8,2,32,2048]{3,2,1,0:T(8,128)(2,1)}, u32[]{:S(2)}, u32[]{:S(2)}) async-start(bf16[8,2,32,2048]{3,2,1,0:T(8,128)(2,1)} %broadcast_in_dim.11), calls=%async_computation.1 | async-start | bytes 4194304 | tf_op jit(solution)/shard_map/all_to_all | solution.py:21
  43.6 2.6 %collective-permute-start.2 = (bf16[256,256]{1,0:T(8,128)(2,1)S(1)}, bf16[256,256]{1,0:T(8,128)(2,1)S(1)}, u32[]{:S(2)}, u32[]{:S(2)}) collective-permute-start(bf16[256,256]{1,0:T(8,128)(2,1)S(1)} %copy-done.2), channel_id=1, source_target_pairs={{0,8},{8,0},{1,9},{9,1},{2,10},{10,2},{3,11},{11,3},{4,12},{12,4},... | collective-permute-start | bytes 393224 | tf_op jit(solution)/shard_map/ppermute | solution.py:68
  46.2 1.9 %collective-permute-start.3 = (f32[2,8,256]{2,1,0:T(8,128)S(1)}, f32[2,8,256]{2,1,0:T(8,128)S(1)}, u32[]{:S(2)}, u32[]{:S(2)}) collective-permute-start(f32[2,8,256]{2,1,0:T(8,128)S(1)} %pad_maximum_fusion.3), channel_id=1, source_target_pairs={{0,8},{8,0},{1,9},{9,1},{2,10},{10,2},{3,11},{11,3},{4,12},{12,4},... | collective-permute-start | bytes 49160 | tf_op jit(solution)/shard_map/ppermute | solution.py:68
  48.1 2.1 %convolution_convert_fusion = bf16[256,4096]{1,0:T(8,128)(2,1)} fusion(bf16[256,256]{1,0:T(8,128)(2,1)S(1)} %copy-done.2, bf16[4096,256]{1,0:T(8,128)(2,1)S(1)} %copy-done.1), kind=kOutput, calls=%fused_computation | convolution fusion | flops 537919488 | bytes 4325376 | tf_op jit(solution)/shard_map/dot_general | solution.py:78
  50.3 17.2 %all-gather.2.cloned.1.call-done = bf16[2048,512]{1,0:T(8,128)(2,1)} async-done(((bf16[256,512]{1,0:T(8,128)(2,1)}), bf16[2048,512]{1,0:T(8,128)(2,1)}) %all-gather.2.cloned.1.call-update) | async-done | bytes 2097168 | tf_op jit(solution)/shard_map/all_gather | solution.py:72
  67.5 1.6 %copy-done = bf16[2048,512]{1,0:T(8,128)(2,1)S(1)} copy-done((bf16[2048,512]{1,0:T(8,128)(2,1)S(1)}, bf16[2048,512]{1,0:T(8,128)(2,1)}, u32[]{:S(2)}) %copy-start) | copy-done | bytes 2097176
  69.1 6.1 %collective-permute-start.4 = (bf16[2048,512]{1,0:T(8,128)(2,1)S(1)}, bf16[2048,512]{1,0:T(8,128)(2,1)}, u32[]{:S(2)}, u32[]{:S(2)}) collective-permute-start(bf16[2048,512]{1,0:T(8,128)(2,1)S(1)} %copy-done), channel_id=1, source_target_pairs={{0,8},{8,0},{1,9},{9,1},{2,10},{10,2},{3,11},{11,3},{4,12},{12,4},... | collective-permute-start | bytes 6291464 | tf_op jit(solution)/shard_map/ppermute | solution.py:68
  75.1 2.8 %convolution_convert_fusion.1 = bf16[512,512]{1,0:T(8,128)(2,1)S(1)} fusion(bf16[512,2048]{1,0:T(8,128)(2,1)} %bitcast.22, bf16[2048,512]{1,0:T(8,128)(2,1)S(1)} %copy-done), kind=kOutput, calls=%fused_computation.1 | convolution fusion | flops 1074003968 | bytes 4718592 | tf_op jit(solution)/shard_map/dot_general | solution.py:86
  78.0 1.1 fusion
  79.0 10.4 %all-to-all-start.2 = ((bf16[32,16,256]{2,1,0:T(8,128)(2,1)}), bf16[32,16,256]{2,1,0:T(8,128)(2,1)S(1)}, u32[]{:S(2)}, u32[]{:S(2)}) async-start(bf16[32,16,256]{2,1,0:T(8,128)(2,1)} %bitcast.23), calls=%async_computation.3 | async-start | bytes 524288 | tf_op jit(solution)/shard_map/all_to_all | solution.py:90
  89.4 1.7 %slice_select_fusion = bf16[32,1,64,256]{3,2,1,0:T(8,128)(2,1)S(1)} fusion(bf16[32,2,64,256]{3,2,1,0:T(8,128)(2,1)} %bitcast.62, pred[]{:T(512)S(6)} %eq.3), kind=kLoop, calls=%fused_computation.4 | loop fusion | flops 524288 | bytes 3145729 | tf_op jit(solution)/shard_map/jit(_where)/select_n | solution.py:99
  91.1 2.3 %fusion.6 = f32[8,2,32,256]{3,2,1,0:T(8,128)S(1)} fusion(bf16[8,2,32,2048]{3,2,1,0:T(8,128)(2,1)} %all-to-all-done.1, bf16[2048,256,1,1]{1,0,3,2:T(8,128)(2,1)S(1)} %bitcast.64), kind=kOutput, calls=%fused_computation.27 | convolution fusion | flops 536870912 | bytes 3670016 | tf_op jit(solution)/shard_map/dot_general | solution.py:100
  93.4 9.2 %all-to-all-done.2 = bf16[32,16,256]{2,1,0:T(8,128)(2,1)S(1)} async-done(((bf16[32,16,256]{2,1,0:T(8,128)(2,1)}), bf16[32,16,256]{2,1,0:T(8,128)(2,1)S(1)}, u32[]{:S(2)}, u32[]{:S(2)}) %all-to-all-start.2) | async-done | bytes 262176 | tf_op jit(solution)/shard_map/all_to_all | solution.py:90
  102.6 3.6 %collective-permute-start.5 = (f32[16,256]{1,0:T(8,128)S(1)}, f32[16,256]{1,0:T(8,128)S(1)}, u32[]{:S(2)}, u32[]{:S(2)}) collective-permute-start(f32[16,256]{1,0:T(8,128)S(1)} %convert_reduce_fusion), channel_id=1, source_target_pairs={{0,8},{8,0},{1,9},{9,1},{2,10},{10,2},{3,11},{11,3},{4,12},{12,4},... | collective-permute-start | bytes 49160 | tf_op jit(solution)/shard_map/ppermute | solution.py:68
  106.3 1.9 %collective-permute-start.1 = (f32[8,32,256]{2,1,0:T(8,128)S(1)}, f32[8,32,256]{2,1,0:T(8,128)S(1)}, u32[]{:S(2)}, u32[]{:S(2)}) collective-permute-start(f32[8,32,256]{2,1,0:T(8,128)S(1)} %slice_bitcast_fusion), channel_id=1, source_target_pairs={{0,8},{8,0},{1,9},{9,1},{2,10},{10,2},{3,11},{11,3},{4,12},{12,4},... | collective-permute-start | bytes 786440 | tf_op jit(solution)/shard_map/ppermute | solution.py:68
  109.0 4.5 %all-to-all-start.3 = ((bf16[32,16,256]{2,1,0:T(8,128)(2,1)}), bf16[32,16,256]{2,1,0:T(8,128)(2,1)S(1)}, u32[]{:S(2)}, u32[]{:S(2)}) async-start(bf16[32,16,256]{2,1,0:T(8,128)(2,1)} %broadcast_in_dim.28), calls=%async_computation.4 | async-start | bytes 524288 | tf_op jit(solution)/shard_map/all_to_all | solution.py:21
  114.9 11.3 %all-to-all-done.3 = bf16[32,16,256]{2,1,0:T(8,128)(2,1)S(1)} async-done(((bf16[32,16,256]{2,1,0:T(8,128)(2,1)}), bf16[32,16,256]{2,1,0:T(8,128)(2,1)S(1)}, u32[]{:S(2)}, u32[]{:S(2)}) %all-to-all-start.3) | async-done | bytes 262176 | tf_op jit(solution)/shard_map/all_to_all | solution.py:21
  126.1 4.2 %shard_map.101 = bf16[32,2,64,256]{3,2,1,0:T(8,128)(2,1)} custom-call(s32[2]{0:T(128)S(1)} %pad_add_fusion.core_ref, bf16[1,2048,512]{2,1,0:T(8,128)(2,1)S(1)} %bitcast.60, bf16[1,2048,512]{2,1,0:T(8,128)(2,1)} %bitcast.20.other_ref, bf16[512,256]{1,0:T(8,128)(2,1)S(1)} %bitcast.61), custom_call_target="tpu_custom_call" | custom-call | flops 1073741824 | bytes 6291456 | tf_op jit(solution)/shard_map/pallas_call | solution.py:38
  (36 shorter events, 3.7 us)
Async XLA Ops:
  7.2 60.3 %all-gather.2.cloned.1.call-start = ((), (), s32[]{:S(2)}) async-start(), calls=%async_computation.5 | async-start | bytes 2359296 | tf_op jit(solution)/shard_map/all_gather | solution.py:72
  30.6 6.6 %collective-permute-start = (bf16[32,2048]{1,0:T(8,128)(2,1)S(1)}, bf16[32,2048]{1,0:T(8,128)(2,1)S(1)}, u32[]{:S(2)}, u32[]{:S(2)}) collective-permute-start(bf16[32,2048]{1,0:T(8,128)(2,1)S(1)} %select_n.66), channel_id=1, source_target_pairs={{0,8},{8,0},{1,9},{9,1},{2,10},{10,2},{3,11},{11,3},{4,12},{12,4},... | collective-permute-start | bytes 393224 | tf_op jit(solution)/shard_map/ppermute | solution.py:68
  38.8 4.8 %copy-start.2 = (bf16[256,256]{1,0:T(8,128)(2,1)S(1)}, bf16[256,256]{1,0:T(8,128)(2,1)}, u32[]{:S(2)}) copy-start(bf16[256,256]{1,0:T(8,128)(2,1)} %param.8) | copy-start | bytes 393220
  38.8 7.4 %copy-start.3 = (f32[8,256]{1,0:T(8,128)S(1)}, f32[8,256]{1,0:T(8,128)}, u32[]{:S(2)}) copy-start(f32[8,256]{1,0:T(8,128)} %param.11) | copy-start | bytes 24580
  38.8 7.4 %copy-start.4 = (f32[8,256]{1,0:T(8,128)S(1)}, f32[8,256]{1,0:T(8,128)}, u32[]{:S(2)}) copy-start(f32[8,256]{1,0:T(8,128)} %param.10) | copy-start | bytes 24580
  38.8 9.3 %copy-start.1 = (bf16[4096,256]{1,0:T(8,128)(2,1)S(1)}, bf16[4096,256]{1,0:T(8,128)(2,1)}, u32[]{:S(2)}) copy-start(bf16[4096,256]{1,0:T(8,128)(2,1)} %param.7) | copy-start | bytes 6291460
  38.8 36.3 %all-to-all-start.1 = ((bf16[8,2,32,2048]{3,2,1,0:T(8,128)(2,1)}), bf16[8,2,32,2048]{3,2,1,0:T(8,128)(2,1)}, u32[]{:S(2)}, u32[]{:S(2)}) async-start(bf16[8,2,32,2048]{3,2,1,0:T(8,128)(2,1)} %broadcast_in_dim.11), calls=%async_computation.1 | async-start | bytes 4194304 | tf_op jit(solution)/shard_map/all_to_all | solution.py:21
  43.6 86.8 %reduce-scatter.2.cloned.1.call-start = ((), (), s32[]{:S(2)}) async-start(), calls=%async_computation.6 | async-start | bytes 2359296 | tf_op jit(solution)/shard_map/reduce_scatter | solution.py:84
  43.6 6.6 %collective-permute-start.2 = (bf16[256,256]{1,0:T(8,128)(2,1)S(1)}, bf16[256,256]{1,0:T(8,128)(2,1)S(1)}, u32[]{:S(2)}, u32[]{:S(2)}) collective-permute-start(bf16[256,256]{1,0:T(8,128)(2,1)S(1)} %copy-done.2), channel_id=1, source_target_pairs={{0,8},{8,0},{1,9},{9,1},{2,10},{10,2},{3,11},{11,3},{4,12},{12,4},... | collective-permute-start | bytes 393224 | tf_op jit(solution)/shard_map/ppermute | solution.py:68
  46.2 4.0 %collective-permute-start.3 = (f32[2,8,256]{2,1,0:T(8,128)S(1)}, f32[2,8,256]{2,1,0:T(8,128)S(1)}, u32[]{:S(2)}, u32[]{:S(2)}) collective-permute-start(f32[2,8,256]{2,1,0:T(8,128)S(1)} %pad_maximum_fusion.3), channel_id=1, source_target_pairs={{0,8},{8,0},{1,9},{9,1},{2,10},{10,2},{3,11},{11,3},{4,12},{12,4},... | collective-permute-start | bytes 49160 | tf_op jit(solution)/shard_map/ppermute | solution.py:68
  67.5 1.6 %copy-start = (bf16[2048,512]{1,0:T(8,128)(2,1)S(1)}, bf16[2048,512]{1,0:T(8,128)(2,1)}, u32[]{:S(2)}) copy-start(bf16[2048,512]{1,0:T(8,128)(2,1)} %all-gather.2.cloned.1.call-done) | copy-start | bytes 6291460
  69.1 57.1 %collective-permute-start.4 = (bf16[2048,512]{1,0:T(8,128)(2,1)S(1)}, bf16[2048,512]{1,0:T(8,128)(2,1)}, u32[]{:S(2)}, u32[]{:S(2)}) collective-permute-start(bf16[2048,512]{1,0:T(8,128)(2,1)S(1)} %copy-done), channel_id=1, source_target_pairs={{0,8},{8,0},{1,9},{9,1},{2,10},{10,2},{3,11},{11,3},{4,12},{12,4},... | collective-permute-start | bytes 6291464 | tf_op jit(solution)/shard_map/ppermute | solution.py:68
  79.0 23.6 %all-to-all-start.2 = ((bf16[32,16,256]{2,1,0:T(8,128)(2,1)}), bf16[32,16,256]{2,1,0:T(8,128)(2,1)S(1)}, u32[]{:S(2)}, u32[]{:S(2)}) async-start(bf16[32,16,256]{2,1,0:T(8,128)(2,1)} %bitcast.23), calls=%async_computation.3 | async-start | bytes 524288 | tf_op jit(solution)/shard_map/all_to_all | solution.py:90
  102.6 5.6 %collective-permute-start.5 = (f32[16,256]{1,0:T(8,128)S(1)}, f32[16,256]{1,0:T(8,128)S(1)}, u32[]{:S(2)}, u32[]{:S(2)}) collective-permute-start(f32[16,256]{1,0:T(8,128)S(1)} %convert_reduce_fusion), channel_id=1, source_target_pairs={{0,8},{8,0},{1,9},{9,1},{2,10},{10,2},{3,11},{11,3},{4,12},{12,4},... | collective-permute-start | bytes 49160 | tf_op jit(solution)/shard_map/ppermute | solution.py:68
  106.3 7.3 %collective-permute-start.1 = (f32[8,32,256]{2,1,0:T(8,128)S(1)}, f32[8,32,256]{2,1,0:T(8,128)S(1)}, u32[]{:S(2)}, u32[]{:S(2)}) collective-permute-start(f32[8,32,256]{2,1,0:T(8,128)S(1)} %slice_bitcast_fusion), channel_id=1, source_target_pairs={{0,8},{8,0},{1,9},{9,1},{2,10},{10,2},{3,11},{11,3},{4,12},{12,4},... | collective-permute-start | bytes 786440 | tf_op jit(solution)/shard_map/ppermute | solution.py:68
  109.0 17.2 %all-to-all-start.3 = ((bf16[32,16,256]{2,1,0:T(8,128)(2,1)}), bf16[32,16,256]{2,1,0:T(8,128)(2,1)S(1)}, u32[]{:S(2)}, u32[]{:S(2)}) async-start(bf16[32,16,256]{2,1,0:T(8,128)(2,1)} %broadcast_in_dim.28), calls=%async_computation.4 | async-start | bytes 524288 | tf_op jit(solution)/shard_map/all_to_all | solution.py:21
Sparse Core Ops, SparseCore 0:
  27.7 39.7 all-gather.1
  70.9 54.8 reduce-scatter.1

commit v3 on v2

--- a/solution.py
+++ b/solution.py
@@ -24,7 +24,7 @@
 def update_rows(cores, basis_own, basis_other, step, rows):
     parts, half, width = basis_own.shape
     heads = step.shape[1]
-    blocks = 4
+    blocks = 16
 
     def kernel(core_ref, own_ref, other_ref, step_ref, out_ref):
         for ref, place in ((own_ref, core_ref[0]), (other_ref, core_ref[1])):
@@ -75,32 +75,42 @@
     x_own, x_other = (v.reshape(own_tokens, half) for v in ordered(x_split[:, :, 0], x_split[:, :, 1]))
     both_x = copies_to(jnp.stack([x_own, swap(x_other)]), TENSOR, 8).reshape(2 * tokens, half)
 
-    terms = lax.dot_general(grad_out, weight, (((1,), (1,)), ((), ())), preferred_element_type=f32).astype(bf16)
+    by_x = grad_out.reshape(2, 4, own_tokens, heads).transpose(1, 0, 2, 3).reshape(tokens, heads)
+    terms = lax.dot_general(by_x, weight, (((1,), (1,)), ((), ())), preferred_element_type=f32).astype(bf16)
     grads = [g.reshape(8, own_tokens, heads) for g in (grad_out, swap(grad_out))]
     both_grads = jnp.stack(grads, axis=1).reshape(2 * tokens, heads)
     moments = jnp.stack([moment1, moment2])
     moments = jnp.stack(ordered(moments, swap(moments)), axis=1).reshape(2, 2 * moment1.shape[0], heads)
-    proj_own, terms, both_grads, moments = lax.optimization_barrier((proj_own, terms, both_grads, moments))
-    grad_in = lax.psum_scatter(terms, TENSOR, scatter_dimension=0, tiled=True)
+    w_split = weight.reshape(count, 2, rows, heads)
+    w_own = jnp.where(first, w_split[:, 0], w_split[:, 1]).reshape(half, heads)
+    proj_own, terms, both_grads, moments, w_own = lax.optimization_barrier(
+        (proj_own, terms, both_grads, moments, w_own)
+    )
+    met = lax.psum_scatter(terms, "x", scatter_dimension=0, tiled=True)
 
     projected = jnp.dot(both_x, proj_own, preferred_element_type=f32).astype(bf16)
-    projected = lax.optimization_barrier(projected)
+    projected, proj_own = lax.optimization_barrier((projected, proj_own))
     local = lax.dot_general(projected, both_grads, dims, preferred_element_type=f32)
     local = (local * (1.0 / math.sqrt(tokens))).astype(bf16).reshape(count, -1, heads)
     chip = jnp.sum(lax.all_to_all(local, RING, 0, 0, tiled=True).astype(f32), axis=0)
+    parts = jnp.dot(both_x, w_own, preferred_element_type=f32).reshape(8, 2, own_tokens, heads)
+    chip, theirs = lax.optimization_barrier((chip, swap(parts[:, 1])))
+    values = (parts[:, 0] + theirs).astype(bf16).reshape(tokens, heads)
+
     coeff = chip + swap(chip)
     both1 = 0.9 * moments[0] + 0.1 * coeff
     both2 = 0.999 * moments[1] + 0.001 * coeff * coeff
     step_dir = both1 / (1.0 - 0.9**10) / (jnp.sqrt(both2 / (1.0 - 0.999**10)) + 1e-08)
     new_moment1, new_moment2 = (jnp.where(first, m[:8], m[8:]) for m in (both1, both2))
+    proj_other = swap(proj_own)
+    step = copies_to(step_dir.astype(bf16), RING, count).reshape(rank, heads)
 
-    proj_other = swap(proj_own)
-    w_split = weight.reshape(count, 2, rows, heads)
-    w_own = jnp.where(first, w_split[:, 0], w_split[:, 1]).reshape(half, heads)
-    parts = jnp.dot(both_x, w_own, preferred_element_type=f32).reshape(8, 2, own_tokens, heads)
-    values = (parts[:, 0] + swap(parts[:, 1])).astype(bf16).reshape(tokens, heads)
-
-    step = copies_to(step_dir.astype(bf16), RING, count).reshape(rank, heads)
+    new_moment1, met = lax.optimization_barrier((new_moment1, met))
+    met = met.reshape(2, own_tokens, features)
+    zl = lax.axis_index("zl")
+    far = lax.ppermute(lax.dynamic_index_in_dim(met, 1 - zl, axis=0, keepdims=False), "zl", SWAP)
+    near = lax.dynamic_index_in_dim(met, zl, axis=0, keepdims=False)
+    grad_in = (near.astype(f32) + far.astype(f32)).astype(bf16)
     update = update_rows(jnp.stack([core, 1 - core]), proj_own[None], proj_other[None], step, rows)
     return (values, grad_in, update, new_moment1, new_moment2)
 

time: 139 us -> 140 us (level)
  waiting for transfers between devices: 38.4 us -> 27.8 us
  starting transfers between devices: 41.4 us -> 49.2 us
  other arithmetic: 3.25 us -> 5.53 us
    all_to_all x1, waiting for transfers between devices: 9.21 us -> 0.01 us  [per_device(): lax.all_to_all(local, RING, 0, 0, tiled=True).astype(f32)]
    all_to_all x2, starting transfers between devices: 9.26 us -> 12.6 us  [copies_to(): return lax.all_to_all(copies, axes, 0, 0, tiled=True)]
    ppermute x6, starting transfers between devices: 21.7 us -> 24.7 us  [swap(): return lax.ppermute(value, 'c', SWAP)]
    ppermute x0 -> x1, starting transfers between devices: none -> 2.36 us  [per_device(): lax.ppermute(lax.dynamic_index_in_dim(met, 1 - zl, axis=0, keepdims=False...]
    all_gather x1, waiting for transfers between devices: 17.2 us -> 15.1 us  [per_device(): lax.all_gather(proj_z.reshape(4 * rows, rank), 'y', axis=0, tiled=True)]
    convert_element_type x1 -> x2, other arithmetic: 0.68 us -> 2.42 us  [the longest x1 1.65 us: per_device(): values = (parts[:, 0] + theirs).astype(bf16).reshape(tokens, heads)]
    select_n x1, other arithmetic: 1.66 us -> 0.11 us  [per_device(): w_own = jnp.where(first, w_split[:, 0], w_split[:, 1]).reshape(half, heads)]
  transfers between devices with their start and end apart: 11 -> 12, of which waited for: 4 -> 5; matrix products, arithmetic and copies ran while one was open for 12% -> 14% of each run, Pallas kernels for 3% -> 3%
where the time goes in v3:
time: 140 us; the launch traced here: 137 us
  starting transfers between devices  49.2 us (35%)
  waiting for transfers between devices  27.8 us (20%)
  blocking collectives  19.5 us (14%)
  between operations  14.3 us (10%)
  local copies, waits for them, and re-layouts  8.65 us (6%)
  matrix products  8.24 us (6%)
  other arithmetic  5.53 us (4%)
  Pallas kernels  4.23 us (3%)
    ppermute x6, starting transfers between devices, swap(): return lax.ppermute(value, 'c', SWAP)  24.7 us
    all_to_all x1, blocking collectives, copies_to(): return lax.all_to_all(copies, axes, 0, 0, tiled=True)  19.5 us
    all_gather x1, waiting for transfers between devices, per_device(): lax.all_gather(proj_z.reshape(4 * rows, rank), 'y', axis=0, tiled=True)  15.1 us
    all_to_all x2, starting transfers between devices, copies_to(): return lax.all_to_all(copies, axes, 0, 0, tiled=True)  12.6 us
    all_to_all x2, waiting for transfers between devices, copies_to(): return lax.all_to_all(copies, axes, 0, 0, tiled=True)  10.5 us
    all_to_all x1, starting transfers between devices, per_device(): lax.all_to_all(local, RING, 0, 0, tiled=True).astype(f32)  9.44 us
    pallas_call x1, Pallas kernels, update_rows(): pl.pallas_call(kernel, out_shape=jax.ShapeDtypeStruct((half // rows, 2, r...  4.23 us
    broadcast_in_dim x3, local copies, waits for them, and re-layouts, copies_to(): copies = jnp.broadcast_to(value[None], (count, *value.shape))  3.16 us
  transfers between devices with their start and end apart: 12, of which 5 were waited for; matrix products, arithmetic and copies ran while one was open for 14% of the time, Pallas kernels for 3%

profile of v3, /device:TPU:1, one launch (start us, length us, event | category | flops | bytes accessed | tf_op | source)
XLA Modules:
  0.0 137.4 jit_solution(4886056211296241317)
XLA Ops:
  8.1 19.5 %all_to_all.20 = bf16[4,64,512]{2,1,0:T(8,128)(2,1)} all-to-all(bf16[4,64,512]{2,1,0:T(8,128)(2,1)S(1)} %broadcast_in_dim.10), channel_id=1, replica_groups=mesh['y'=8,'zh'=4,'c'=2,'zl'=2,'x'=4] {'zh'}, dimensions={0} | all-to-all | bytes 524288 | tf_op jit(solution)/shard_map/all_to_all | solution.py:21
  27.6 1.5 %reshape.90 = bf16[32,32,2,64]{3,2,1,0:T(2,128)(2,1)S(1)} reshape(bf16[32,4096]{1,0:T(8,128)(2,1)} %param.6) | data formatting | bytes 524288 | tf_op jit(solution)/shard_map/reshape | solution.py:74
  29.1 1.2 fusion.8
  30.6 5.6 %collective-permute-start = (bf16[32,2048]{1,0:T(8,128)(2,1)S(1)}, bf16[32,2048]{1,0:T(8,128)(2,1)S(1)}, u32[]{:S(2)}, u32[]{:S(2)}) collective-permute-start(bf16[32,2048]{1,0:T(8,128)(2,1)S(1)} %select_n.73), channel_id=1, source_target_pairs={{0,8},{8,0},{1,9},{9,1},{2,10},{10,2},{3,11},{11,3},{4,12},{12,4},... | collective-permute-start | bytes 393224 | tf_op jit(solution)/shard_map/ppermute | solution.py:68
  37.2 1.6 %broadcast_in_dim.11 = bf16[8,2,32,2048]{3,2,1,0:T(8,128)(2,1)} broadcast(bf16[2,32,2048]{2,1,0:T(8,128)(2,1)S(1)} %pad_maximum_fusion), dimensions={1,2,3} | broadcast | bytes 2359296 | tf_op jit(solution)/shard_map/broadcast_in_dim | solution.py:20
  38.8 4.7 %all-to-all-start.1 = ((bf16[8,2,32,2048]{3,2,1,0:T(8,128)(2,1)}), bf16[8,2,32,2048]{3,2,1,0:T(8,128)(2,1)}, u32[]{:S(2)}, u32[]{:S(2)}) async-start(bf16[8,2,32,2048]{3,2,1,0:T(8,128)(2,1)} %broadcast_in_dim.11), calls=%async_computation.1 | async-start | bytes 4194304 | tf_op jit(solution)/shard_map/all_to_all | solution.py:21
  44.3 2.5 %collective-permute-start.2 = (f32[2,8,256]{2,1,0:T(8,128)S(1)}, f32[2,8,256]{2,1,0:T(8,128)S(1)}, u32[]{:S(2)}, u32[]{:S(2)}) collective-permute-start(f32[2,8,256]{2,1,0:T(8,128)S(1)} %pad_maximum_fusion.3), channel_id=1, source_target_pairs={{0,8},{8,0},{1,9},{9,1},{2,10},{10,2},{3,11},{11,3},{4,12},{12,4},... | collective-permute-start | bytes 49160 | tf_op jit(solution)/shard_map/ppermute | solution.py:68
  46.8 1.9 %collective-permute-start.1 = (bf16[256,256]{1,0:T(8,128)(2,1)S(1)}, bf16[256,256]{1,0:T(8,128)(2,1)}, u32[]{:S(2)}, u32[]{:S(2)}) collective-permute-start(bf16[256,256]{1,0:T(8,128)(2,1)S(1)} %copy-done.4), channel_id=1, source_target_pairs={{0,8},{8,0},{1,9},{9,1},{2,10},{10,2},{3,11},{11,3},{4,12},{12,4},... | collective-permute-start | bytes 393224 | tf_op jit(solution)/shard_map/ppermute | solution.py:68
  48.8 2.1 %convolution_convert_fusion = bf16[256,4096]{1,0:T(8,128)(2,1)} fusion(bf16[256,256]{1,0:T(8,128)(2,1)S(1)} %bitcast.76, bf16[4096,256]{1,0:T(8,128)(2,1)S(1)} %copy-done.1), kind=kOutput, calls=%fused_computation | convolution fusion | flops 537919488 | bytes 4325376 | tf_op jit(solution)/shard_map/dot_general | solution.py:79
  52.4 15.1 %all-gather.2.cloned.1.call-done = bf16[2048,512]{1,0:T(8,128)(2,1)} async-done(((bf16[256,512]{1,0:T(8,128)(2,1)}), bf16[2048,512]{1,0:T(8,128)(2,1)}) %all-gather.2.cloned.1.call-update) | async-done | bytes 2097168 | tf_op jit(solution)/shard_map/all_gather | solution.py:72
  67.5 2.3 %all-to-all-done.1 = bf16[8,2,32,2048]{3,2,1,0:T(8,128)(2,1)} async-done(((bf16[8,2,32,2048]{3,2,1,0:T(8,128)(2,1)}), bf16[8,2,32,2048]{3,2,1,0:T(8,128)(2,1)}, u32[]{:S(2)}, u32[]{:S(2)}) %all-to-all-start.1) | async-done | bytes 2097184 | tf_op jit(solution)/shard_map/all_to_all | solution.py:21
  69.8 2.8 %convolution_convert_fusion.1 = bf16[512,512]{1,0:T(8,128)(2,1)S(1)} fusion(bf16[512,2048]{1,0:T(8,128)(2,1)} %bitcast.18, bf16[2048,512]{1,0:T(8,128)(2,1)S(1)} %copy-done), kind=kOutput, calls=%fused_computation.1 | convolution fusion | flops 1074003968 | bytes 4718592 | tf_op jit(solution)/shard_map/dot_general | solution.py:91
  72.7 1.1 fusion
  73.7 9.4 %all-to-all-start.2 = ((bf16[32,16,256]{2,1,0:T(8,128)(2,1)}), bf16[32,16,256]{2,1,0:T(8,128)(2,1)S(1)}, u32[]{:S(2)}, u32[]{:S(2)}) async-start(bf16[32,16,256]{2,1,0:T(8,128)(2,1)} %bitcast.81), calls=%async_computation.2 | async-start | bytes 524288 | tf_op jit(solution)/shard_map/all_to_all | solution.py:95
  83.2 6.5 %collective-permute-start.6 = (bf16[2048,512]{1,0:T(8,128)(2,1)S(1)}, bf16[2048,512]{1,0:T(8,128)(2,1)}, u32[]{:S(2)}, u32[]{:S(2)}) collective-permute-start(bf16[2048,512]{1,0:T(8,128)(2,1)S(1)} %copy-done), channel_id=1, source_target_pairs={{0,8},{8,0},{1,9},{9,1},{2,10},{10,2},{3,11},{11,3},{4,12},{12,4},... | collective-permute-start | bytes 6291464 | tf_op jit(solution)/shard_map/ppermute | solution.py:68
  89.7 2.3 %fusion.1 = f32[8,2,32,256]{3,2,1,0:T(8,128)S(1)} fusion(bf16[8,2,32,2048]{3,2,1,0:T(8,128)(2,1)} %all-to-all-done.1, bf16[2048,256]{1,0:T(8,128)(2,1)S(1)} %bitcast.74), kind=kOutput, calls=%fused_computation.5 | convolution fusion | flops 536870912 | bytes 3670016 | tf_op jit(solution)/shard_map/dot_general | solution.py:96
  92.8 1.9 %collective-permute-start.3 = (f32[8,32,256]{2,1,0:T(8,128)S(1)}, f32[8,32,256]{2,1,0:T(8,128)S(1)}, u32[]{:S(2)}, u32[]{:S(2)}) collective-permute-start(f32[8,32,256]{2,1,0:T(8,128)S(1)} %slice_bitcast_fusion), channel_id=1, source_target_pairs={{0,8},{8,0},{1,9},{9,1},{2,10},{10,2},{3,11},{11,3},{4,12},{12,4},... | collective-permute-start | bytes 786440 | tf_op jit(solution)/shard_map/ppermute | solution.py:68
  94.9 1.4 collective-permute-done.3
  96.2 6.2 %collective-permute-start.4 = (f32[16,256]{1,0:T(8,128)S(1)}, f32[16,256]{1,0:T(8,128)S(1)}, u32[]{:S(2)}, u32[]{:S(2)}) collective-permute-start(f32[16,256]{1,0:T(8,128)S(1)} %convert_reduce_fusion), channel_id=1, source_target_pairs={{0,8},{8,0},{1,9},{9,1},{2,10},{10,2},{3,11},{11,3},{4,12},{12,4},... | collective-permute-start | bytes 49160 | tf_op jit(solution)/shard_map/ppermute | solution.py:68
  102.5 1.7 %fusion.5 = bf16[8,32,256]{2,1,0:T(8,128)(2,1)} fusion(f32[8,32,256]{2,1,0:T(8,128)S(1)} %collective-permute-done.3, f32[8,2,32,256]{3,2,1,0:T(8,128)} %copy-done.3), kind=kLoop, calls=%fused_computation.13 | loop fusion | flops 131072 | bytes 655360 | tf_op jit(solution)/shard_map/convert_element_type | solution.py:98
  104.9 7.8 %all-to-all-start.3 = ((bf16[32,16,256]{2,1,0:T(8,128)(2,1)}), bf16[32,16,256]{2,1,0:T(8,128)(2,1)S(1)}, u32[]{:S(2)}, u32[]{:S(2)}) async-start(bf16[32,16,256]{2,1,0:T(8,128)(2,1)} %broadcast_in_dim.28), calls=%async_computation.4 | async-start | bytes 524288 | tf_op jit(solution)/shard_map/all_to_all | solution.py:21
  114.3 2.4 %collective-permute-start.5 = (bf16[32,4096]{1,0:T(8,128)(2,1)S(1)}, bf16[32,4096]{1,0:T(8,128)(2,1)S(1)}, u32[]{:S(2)}, u32[]{:S(2)}) collective-permute-start(bf16[32,4096]{1,0:T(8,128)(2,1)S(1)} %dynamic-slice_bitcast_fusion), channel_id=1, source_target_pairs={{0,4},{4,0},{1,5},{5,1},{2,6},{6,2},{3,7},{7,3},{8,12},{12,8},{9,1... | collective-permute-start | bytes 786440 | tf_op jit(solution)/shard_map/ppermute | solution.py:111
  117.3 8.2 %all-to-all-done.3 = bf16[32,16,256]{2,1,0:T(8,128)(2,1)S(1)} async-done(((bf16[32,16,256]{2,1,0:T(8,128)(2,1)}), bf16[32,16,256]{2,1,0:T(8,128)(2,1)S(1)}, u32[]{:S(2)}, u32[]{:S(2)}) %all-to-all-start.3) | async-done | bytes 262176 | tf_op jit(solution)/shard_map/all_to_all | solution.py:21
  125.5 4.2 %shard_map.101 = bf16[32,2,64,256]{3,2,1,0:T(8,128)(2,1)} custom-call(s32[2]{0:T(128)S(1)} %pad_add_fusion.core_ref, bf16[1,2048,512]{2,1,0:T(8,128)(2,1)S(1)} %bitcast.70, bf16[1,2048,512]{2,1,0:T(8,128)(2,1)} %bitcast.29.other_ref, bf16[512,256]{1,0:T(8,128)(2,1)S(1)} %bitcast.71), custom_call_target="tpu_custom_call" | custom-call | flops 1073741824 | bytes 6291456 | tf_op jit(solution)/shard_map/pallas_call | solution.py:38
  (48 shorter events, 9.1 us)
Async XLA Ops:
  7.2 60.3 %all-gather.2.cloned.1.call-start = ((), (), s32[]{:S(2)}) async-start(), calls=%async_computation.5 | async-start | bytes 2359296 | tf_op jit(solution)/shard_map/all_gather | solution.py:72
  30.6 6.6 %collective-permute-start = (bf16[32,2048]{1,0:T(8,128)(2,1)S(1)}, bf16[32,2048]{1,0:T(8,128)(2,1)S(1)}, u32[]{:S(2)}, u32[]{:S(2)}) collective-permute-start(bf16[32,2048]{1,0:T(8,128)(2,1)S(1)} %select_n.73), channel_id=1, source_target_pairs={{0,8},{8,0},{1,9},{9,1},{2,10},{10,2},{3,11},{11,3},{4,12},{12,4},... | collective-permute-start | bytes 393224 | tf_op jit(solution)/shard_map/ppermute | solution.py:68
  38.8 4.8 %copy-start.1 = (bf16[4096,256]{1,0:T(8,128)(2,1)S(1)}, bf16[4096,256]{1,0:T(8,128)(2,1)}, u32[]{:S(2)}) copy-start(bf16[4096,256]{1,0:T(8,128)(2,1)} %param.7) | copy-start | bytes 6291460
  38.8 31.0 %all-to-all-start.1 = ((bf16[8,2,32,2048]{3,2,1,0:T(8,128)(2,1)}), bf16[8,2,32,2048]{3,2,1,0:T(8,128)(2,1)}, u32[]{:S(2)}, u32[]{:S(2)}) async-start(bf16[8,2,32,2048]{3,2,1,0:T(8,128)(2,1)} %broadcast_in_dim.11), calls=%async_computation.1 | async-start | bytes 4194304 | tf_op jit(solution)/shard_map/all_to_all | solution.py:21
  43.5 0.7 copy-start.6
  43.5 0.7 copy-start.7
  43.6 3.3 %copy-start.4 = (bf16[256,256]{1,0:T(8,128)(2,1)S(1)}, bf16[256,256]{1,0:T(8,128)(2,1)}, u32[]{:S(2)}) copy-start(bf16[256,256]{1,0:T(8,128)(2,1)} %param.8) | copy-start | bytes 393220
  43.6 69.8 %reduce-scatter.2.cloned.1.call-start = ((), (), s32[]{:S(2)}) async-start(), calls=%async_computation.6 | async-start | bytes 2621440 | tf_op jit(solution)/shard_map/reduce_scatter | solution.py:89
  44.3 6.6 %collective-permute-start.2 = (f32[2,8,256]{2,1,0:T(8,128)S(1)}, f32[2,8,256]{2,1,0:T(8,128)S(1)}, u32[]{:S(2)}, u32[]{:S(2)}) collective-permute-start(f32[2,8,256]{2,1,0:T(8,128)S(1)} %pad_maximum_fusion.3), channel_id=1, source_target_pairs={{0,8},{8,0},{1,9},{9,1},{2,10},{10,2},{3,11},{11,3},{4,12},{12,4},... | collective-permute-start | bytes 49160 | tf_op jit(solution)/shard_map/ppermute | solution.py:68
  46.8 4.6 %collective-permute-start.1 = (bf16[256,256]{1,0:T(8,128)(2,1)S(1)}, bf16[256,256]{1,0:T(8,128)(2,1)}, u32[]{:S(2)}, u32[]{:S(2)}) collective-permute-start(bf16[256,256]{1,0:T(8,128)(2,1)S(1)} %copy-done.4), channel_id=1, source_target_pairs={{0,8},{8,0},{1,9},{9,1},{2,10},{10,2},{3,11},{11,3},{4,12},{12,4},... | collective-permute-start | bytes 393224 | tf_op jit(solution)/shard_map/ppermute | solution.py:68
  67.5 2.4 %copy-start = (bf16[2048,512]{1,0:T(8,128)(2,1)S(1)}, bf16[2048,512]{1,0:T(8,128)(2,1)}, u32[]{:S(2)}) copy-start(bf16[2048,512]{1,0:T(8,128)(2,1)} %all-gather.2.cloned.1.call-done) | copy-start | bytes 6291460
  73.7 21.1 %all-to-all-start.2 = ((bf16[32,16,256]{2,1,0:T(8,128)(2,1)}), bf16[32,16,256]{2,1,0:T(8,128)(2,1)S(1)}, u32[]{:S(2)}, u32[]{:S(2)}) async-start(bf16[32,16,256]{2,1,0:T(8,128)(2,1)} %bitcast.81), calls=%async_computation.2 | async-start | bytes 524288 | tf_op jit(solution)/shard_map/all_to_all | solution.py:95
  83.2 21.0 %copy-start.5 = (f32[2,16,256]{2,1,0:T(8,128)S(1)}, f32[2,16,256]{2,1,0:T(8,128)}, u32[]{:S(2)}) copy-start(f32[2,16,256]{2,1,0:T(8,128)} %copy_bitcast_fusion) | copy-start | bytes 98308
  83.2 42.3 %collective-permute-start.6 = (bf16[2048,512]{1,0:T(8,128)(2,1)S(1)}, bf16[2048,512]{1,0:T(8,128)(2,1)}, u32[]{:S(2)}, u32[]{:S(2)}) collective-permute-start(bf16[2048,512]{1,0:T(8,128)(2,1)S(1)} %copy-done), channel_id=1, source_target_pairs={{0,8},{8,0},{1,9},{9,1},{2,10},{10,2},{3,11},{11,3},{4,12},{12,4},... | collective-permute-start | bytes 6291464 | tf_op jit(solution)/shard_map/ppermute | solution.py:68
  92.0 0.8 copy-start.3
  92.8 3.4 %collective-permute-start.3 = (f32[8,32,256]{2,1,0:T(8,128)S(1)}, f32[8,32,256]{2,1,0:T(8,128)S(1)}, u32[]{:S(2)}, u32[]{:S(2)}) collective-permute-start(f32[8,32,256]{2,1,0:T(8,128)S(1)} %slice_bitcast_fusion), channel_id=1, source_target_pairs={{0,8},{8,0},{1,9},{9,1},{2,10},{10,2},{3,11},{11,3},{4,12},{12,4},... | collective-permute-start | bytes 786440 | tf_op jit(solution)/shard_map/ppermute | solution.py:68
  96.2 7.9 %collective-permute-start.4 = (f32[16,256]{1,0:T(8,128)S(1)}, f32[16,256]{1,0:T(8,128)S(1)}, u32[]{:S(2)}, u32[]{:S(2)}) collective-permute-start(f32[16,256]{1,0:T(8,128)S(1)} %convert_reduce_fusion), channel_id=1, source_target_pairs={{0,8},{8,0},{1,9},{9,1},{2,10},{10,2},{3,11},{11,3},{4,12},{12,4},... | collective-permute-start | bytes 49160 | tf_op jit(solution)/shard_map/ppermute | solution.py:68
  104.9 20.6 %all-to-all-start.3 = ((bf16[32,16,256]{2,1,0:T(8,128)(2,1)}), bf16[32,16,256]{2,1,0:T(8,128)(2,1)S(1)}, u32[]{:S(2)}, u32[]{:S(2)}) async-start(bf16[32,16,256]{2,1,0:T(8,128)(2,1)} %broadcast_in_dim.28), calls=%async_computation.4 | async-start | bytes 524288 | tf_op jit(solution)/shard_map/all_to_all | solution.py:21
  114.3 15.4 %collective-permute-start.5 = (bf16[32,4096]{1,0:T(8,128)(2,1)S(1)}, bf16[32,4096]{1,0:T(8,128)(2,1)S(1)}, u32[]{:S(2)}, u32[]{:S(2)}) collective-permute-start(bf16[32,4096]{1,0:T(8,128)(2,1)S(1)} %dynamic-slice_bitcast_fusion), channel_id=1, source_target_pairs={{0,4},{4,0},{1,5},{5,1},{2,6},{6,2},{3,7},{7,3},{8,12},{12,8},{9,1... | collective-permute-start | bytes 786440 | tf_op jit(solution)/shard_map/ppermute | solution.py:111
  125.5 4.2 %copy-start.2 = (bf16[64,4096]{1,0:T(8,128)(2,1)S(1)}, bf16[64,4096]{1,0:T(8,128)(2,1)}, u32[]{:S(2)}) copy-start(bf16[64,4096]{1,0:T(8,128)(2,1)} %reduce-scatter.2.cloned.1.call-done) | copy-start | bytes 1572868
Sparse Core Ops, SparseCore 0:
  27.7 39.7 all-gather.1
  70.3 37.7 reduce-scatter.1

commit v4 on v3

--- a/solution.py
+++ b/solution.py
@@ -79,31 +79,26 @@
     terms = lax.dot_general(by_x, weight, (((1,), (1,)), ((), ())), preferred_element_type=f32).astype(bf16)
     grads = [g.reshape(8, own_tokens, heads) for g in (grad_out, swap(grad_out))]
     both_grads = jnp.stack(grads, axis=1).reshape(2 * tokens, heads)
-    moments = jnp.stack([moment1, moment2])
-    moments = jnp.stack(ordered(moments, swap(moments)), axis=1).reshape(2, 2 * moment1.shape[0], heads)
     w_split = weight.reshape(count, 2, rows, heads)
     w_own = jnp.where(first, w_split[:, 0], w_split[:, 1]).reshape(half, heads)
-    proj_own, terms, both_grads, moments, w_own = lax.optimization_barrier(
-        (proj_own, terms, both_grads, moments, w_own)
-    )
+    proj_own, terms, both_grads, w_own = lax.optimization_barrier((proj_own, terms, both_grads, w_own))
     met = lax.psum_scatter(terms, "x", scatter_dimension=0, tiled=True)
 
     projected = jnp.dot(both_x, proj_own, preferred_element_type=f32).astype(bf16)
-    projected, proj_own = lax.optimization_barrier((projected, proj_own))
+    projected = lax.optimization_barrier(projected)
     local = lax.dot_general(projected, both_grads, dims, preferred_element_type=f32)
-    local = (local * (1.0 / math.sqrt(tokens))).astype(bf16).reshape(count, -1, heads)
-    chip = jnp.sum(lax.all_to_all(local, RING, 0, 0, tiled=True).astype(f32), axis=0)
+    local = (local * (1.0 / math.sqrt(tokens))).astype(bf16).reshape(2 * count, -1, heads)
+    coeff = jnp.sum(lax.all_to_all(local, DP, 0, 0, tiled=True).astype(f32), axis=0)
+
     parts = jnp.dot(both_x, w_own, preferred_element_type=f32).reshape(8, 2, own_tokens, heads)
-    chip, theirs = lax.optimization_barrier((chip, swap(parts[:, 1])))
+    coeff, theirs, proj_own = lax.optimization_barrier((coeff, swap(parts[:, 1]), proj_own))
     values = (parts[:, 0] + theirs).astype(bf16).reshape(tokens, heads)
 
-    coeff = chip + swap(chip)
-    both1 = 0.9 * moments[0] + 0.1 * coeff
-    both2 = 0.999 * moments[1] + 0.001 * coeff * coeff
-    step_dir = both1 / (1.0 - 0.9**10) / (jnp.sqrt(both2 / (1.0 - 0.999**10)) + 1e-08)
-    new_moment1, new_moment2 = (jnp.where(first, m[:8], m[8:]) for m in (both1, both2))
+    new_moment1 = 0.9 * moment1 + 0.1 * coeff
+    new_moment2 = 0.999 * moment2 + 0.001 * coeff * coeff
+    step_dir = new_moment1 / (1.0 - 0.9**10) / (jnp.sqrt(new_moment2 / (1.0 - 0.999**10)) + 1e-08)
     proj_other = swap(proj_own)
-    step = copies_to(step_dir.astype(bf16), RING, count).reshape(rank, heads)
+    step = copies_to(step_dir.astype(bf16), DP, 2 * count).reshape(rank, heads)
 
     new_moment1, met = lax.optimization_barrier((new_moment1, met))
     met = met.reshape(2, own_tokens, features)

time: 140 us -> 140 us (level); the launches traced: 137 us -> 139 us
  waiting for transfers between devices: 27.8 us -> 41 us
  starting transfers between devices: 49.2 us -> 38.6 us
    ppermute x6 -> x4, starting transfers between devices: 24.7 us -> 12.9 us  [swap(): return lax.ppermute(value, 'c', SWAP)]
    all_to_all x1, waiting for transfers between devices: 0.01 us -> 9.84 us  [per_device(): lax.all_to_all(local, DP, 0, 0, tiled=True).astype(f32)]
    all_to_all x1, starting transfers between devices: 9.44 us -> 14.2 us  [per_device(): lax.all_to_all(local, DP, 0, 0, tiled=True).astype(f32)]
    all_to_all x2, starting transfers between devices: 12.6 us -> 9.04 us  [copies_to(): return lax.all_to_all(copies, axes, 0, 0, tiled=True)]
    all_to_all x2, waiting for transfers between devices: 10.5 us -> 12.9 us  [copies_to(): return lax.all_to_all(copies, axes, 0, 0, tiled=True)]
    all_gather x1, waiting for transfers between devices: 15.1 us -> 17.4 us  [per_device(): lax.all_gather(proj_z.reshape(4 * rows, rank), 'y', axis=0, tiled=True)]
  transfers between devices with their start and end apart: 12 -> 10, of which waited for: 5 -> 5; matrix products, arithmetic and copies ran while one was open for 14% -> 13% of each run, Pallas kernels for 3% -> 3%
where the time goes in v4:
time: 140 us; the launch traced here: 139 us
  waiting for transfers between devices  41 us (29%)
  starting transfers between devices  38.6 us (28%)
  blocking collectives  19.5 us (14%)
  between operations  14.2 us (10%)
  local copies, waits for them, and re-layouts  8.84 us (6%)
  matrix products  8.3 us (6%)
  other arithmetic  4.31 us (3%)
  Pallas kernels  4.22 us (3%)
    all_to_all x1, blocking collectives, copies_to(): return lax.all_to_all(copies, axes, 0, 0, tiled=True)  19.5 us
    all_gather x1, waiting for transfers between devices, per_device(): lax.all_gather(proj_z.reshape(4 * rows, rank), 'y', axis=0, tiled=True)  17.4 us
    all_to_all x1, starting transfers between devices, per_device(): lax.all_to_all(local, DP, 0, 0, tiled=True).astype(f32)  14.2 us
    all_to_all x2, waiting for transfers between devices, copies_to(): return lax.all_to_all(copies, axes, 0, 0, tiled=True)  12.9 us
    ppermute x4, starting transfers between devices, swap(): return lax.ppermute(value, 'c', SWAP)  12.9 us
    all_to_all x1, waiting for transfers between devices, per_device(): lax.all_to_all(local, DP, 0, 0, tiled=True).astype(f32)  9.84 us
    all_to_all x2, starting transfers between devices, copies_to(): return lax.all_to_all(copies, axes, 0, 0, tiled=True)  9.04 us
    pallas_call x1, Pallas kernels, update_rows(): pl.pallas_call(kernel, out_shape=jax.ShapeDtypeStruct((half // rows, 2, r...  4.22 us
  transfers between devices with their start and end apart: 10, of which 5 were waited for; matrix products, arithmetic and copies ran while one was open for 13% of the time, Pallas kernels for 3%

profile of v4, /device:TPU:1, one launch (start us, length us, event | category | flops | bytes accessed | tf_op | source)
XLA Modules:
  0.0 139.0 jit_solution(4019187549762684065)
XLA Ops:
  8.1 19.5 %all_to_all.20 = bf16[4,64,512]{2,1,0:T(8,128)(2,1)} all-to-all(bf16[4,64,512]{2,1,0:T(8,128)(2,1)S(1)} %broadcast_in_dim.10), channel_id=1, replica_groups=mesh['y'=8,'zh'=4,'c'=2,'zl'=2,'x'=4] {'zh'}, dimensions={0} | all-to-all | bytes 524288 | tf_op jit(solution)/shard_map/all_to_all | solution.py:21
  27.6 1.5 %reshape.83 = bf16[32,32,2,64]{3,2,1,0:T(2,128)(2,1)S(1)} reshape(bf16[32,4096]{1,0:T(8,128)(2,1)} %param.6) | data formatting | bytes 524288 | tf_op jit(solution)/shard_map/reshape | solution.py:74
  29.1 1.2 fusion.9
  30.6 5.6 %collective-permute-start = (bf16[32,2048]{1,0:T(8,128)(2,1)S(1)}, bf16[32,2048]{1,0:T(8,128)(2,1)S(1)}, u32[]{:S(2)}, u32[]{:S(2)}) collective-permute-start(bf16[32,2048]{1,0:T(8,128)(2,1)S(1)} %select_n.49), channel_id=1, source_target_pairs={{0,8},{8,0},{1,9},{9,1},{2,10},{10,2},{3,11},{11,3},{4,12},{12,4},... | collective-permute-start | bytes 393224 | tf_op jit(solution)/shard_map/ppermute | solution.py:68
  37.2 1.6 %broadcast_in_dim.11 = bf16[8,2,32,2048]{3,2,1,0:T(8,128)(2,1)} broadcast(bf16[2,32,2048]{2,1,0:T(8,128)(2,1)S(1)} %pad_maximum_fusion), dimensions={1,2,3} | broadcast | bytes 2359296 | tf_op jit(solution)/shard_map/broadcast_in_dim | solution.py:20
  38.8 4.7 %all-to-all-start.1 = ((bf16[8,2,32,2048]{3,2,1,0:T(8,128)(2,1)}), bf16[8,2,32,2048]{3,2,1,0:T(8,128)(2,1)}, u32[]{:S(2)}, u32[]{:S(2)}) async-start(bf16[8,2,32,2048]{3,2,1,0:T(8,128)(2,1)} %broadcast_in_dim.11), calls=%async_computation.1 | async-start | bytes 4194304 | tf_op jit(solution)/shard_map/all_to_all | solution.py:21
  44.4 2.5 %collective-permute-start.1 = (bf16[256,256]{1,0:T(8,128)(2,1)S(1)}, bf16[256,256]{1,0:T(8,128)(2,1)}, u32[]{:S(2)}, u32[]{:S(2)}) collective-permute-start(bf16[256,256]{1,0:T(8,128)(2,1)S(1)} %copy-done.4), channel_id=1, source_target_pairs={{0,8},{8,0},{1,9},{9,1},{2,10},{10,2},{3,11},{11,3},{4,12},{12,4},... | collective-permute-start | bytes 393224 | tf_op jit(solution)/shard_map/ppermute | solution.py:68
  47.0 2.1 %convolution_convert_fusion = bf16[256,4096]{1,0:T(8,128)(2,1)} fusion(bf16[256,256]{1,0:T(8,128)(2,1)S(1)} %bitcast.63, bf16[4096,256]{1,0:T(8,128)(2,1)S(1)} %copy-done.1), kind=kOutput, calls=%fused_computation | convolution fusion | flops 537919488 | bytes 4325376 | tf_op jit(solution)/shard_map/dot_general | solution.py:79
  49.1 0.9 pad_maximum_fusion.1
  50.0 17.4 %all-gather.2.cloned.1.call-done = bf16[2048,512]{1,0:T(8,128)(2,1)} async-done(((bf16[256,512]{1,0:T(8,128)(2,1)}), bf16[2048,512]{1,0:T(8,128)(2,1)}) %all-gather.2.cloned.1.call-update) | async-done | bytes 2097168 | tf_op jit(solution)/shard_map/all_gather | solution.py:72
  67.5 2.3 %all-to-all-done.1 = bf16[8,2,32,2048]{3,2,1,0:T(8,128)(2,1)} async-done(((bf16[8,2,32,2048]{3,2,1,0:T(8,128)(2,1)}), bf16[8,2,32,2048]{3,2,1,0:T(8,128)(2,1)}, u32[]{:S(2)}, u32[]{:S(2)}) %all-to-all-start.1) | async-done | bytes 2097184 | tf_op jit(solution)/shard_map/all_to_all | solution.py:21
  69.8 2.8 %convolution_convert_fusion.1 = bf16[512,512]{1,0:T(8,128)(2,1)S(1)} fusion(bf16[512,2048]{1,0:T(8,128)(2,1)} %bitcast.13, bf16[2048,512]{1,0:T(8,128)(2,1)S(1)} %copy-done), kind=kOutput, calls=%fused_computation.1 | convolution fusion | flops 1074003968 | bytes 4718592 | tf_op jit(solution)/shard_map/dot_general | solution.py:87
  72.7 1.1 fusion.1
  73.7 14.2 %all-to-all-start.2 = ((bf16[64,8,256]{2,1,0:T(8,128)(2,1)}), bf16[64,8,256]{2,1,0:T(8,128)(2,1)S(1)}, u32[]{:S(2)}, u32[]{:S(2)}) async-start(bf16[64,8,256]{2,1,0:T(8,128)(2,1)} %fusion.1), calls=%async_computation.2 | async-start | bytes 524288 | tf_op jit(solution)/shard_map/all_to_all | solution.py:91
  88.0 2.3 %fusion.2 = f32[8,2,32,256]{3,2,1,0:T(8,128)S(1)} fusion(bf16[8,2,32,2048]{3,2,1,0:T(8,128)(2,1)} %all-to-all-done.1, bf16[2048,256]{1,0:T(8,128)(2,1)S(1)} %bitcast.61), kind=kOutput, calls=%fused_computation.6 | convolution fusion | flops 536870912 | bytes 3670016 | tf_op jit(solution)/shard_map/dot_general | solution.py:93
  91.1 2.6 %collective-permute-start.2 = (f32[8,32,256]{2,1,0:T(8,128)S(1)}, f32[8,32,256]{2,1,0:T(8,128)S(1)}, u32[]{:S(2)}, u32[]{:S(2)}) collective-permute-start(f32[8,32,256]{2,1,0:T(8,128)S(1)} %slice_bitcast_fusion), channel_id=1, source_target_pairs={{0,8},{8,0},{1,9},{9,1},{2,10},{10,2},{3,11},{11,3},{4,12},{12,4},... | collective-permute-start | bytes 786440 | tf_op jit(solution)/shard_map/ppermute | solution.py:68
  93.7 9.8 %all-to-all-done.2 = bf16[64,8,256]{2,1,0:T(8,128)(2,1)S(1)} async-done(((bf16[64,8,256]{2,1,0:T(8,128)(2,1)}), bf16[64,8,256]{2,1,0:T(8,128)(2,1)S(1)}, u32[]{:S(2)}, u32[]{:S(2)}) %all-to-all-start.2) | async-done | bytes 262176 | tf_op jit(solution)/shard_map/all_to_all | solution.py:91
  103.6 2.2 %collective-permute-start.4 = (bf16[2048,512]{1,0:T(8,128)(2,1)S(1)}, bf16[2048,512]{1,0:T(8,128)(2,1)}, u32[]{:S(2)}, u32[]{:S(2)}) collective-permute-start(bf16[2048,512]{1,0:T(8,128)(2,1)S(1)} %copy-done), channel_id=1, source_target_pairs={{0,8},{8,0},{1,9},{9,1},{2,10},{10,2},{3,11},{11,3},{4,12},{12,4},... | collective-permute-start | bytes 6291464 | tf_op jit(solution)/shard_map/ppermute | solution.py:68
  107.2 4.3 %all-to-all-start.3 = ((bf16[64,8,256]{2,1,0:T(8,128)(2,1)}), bf16[64,8,256]{2,1,0:T(8,128)(2,1)S(1)}, u32[]{:S(2)}, u32[]{:S(2)}) async-start(bf16[64,8,256]{2,1,0:T(8,128)(2,1)} %broadcast_in_dim.28), calls=%async_computation.4 | async-start | bytes 524288 | tf_op jit(solution)/shard_map/all_to_all | solution.py:21
  111.5 1.0 dynamic-slice_bitcast_fusion
  112.5 2.4 %collective-permute-start.3 = (bf16[32,4096]{1,0:T(8,128)(2,1)S(1)}, bf16[32,4096]{1,0:T(8,128)(2,1)S(1)}, u32[]{:S(2)}, u32[]{:S(2)}) collective-permute-start(bf16[32,4096]{1,0:T(8,128)(2,1)S(1)} %dynamic-slice_bitcast_fusion), channel_id=1, source_target_pairs={{0,4},{4,0},{1,5},{5,1},{2,6},{6,2},{3,7},{7,3},{8,12},{12,8},{9,1... | collective-permute-start | bytes 786440 | tf_op jit(solution)/shard_map/ppermute | solution.py:106
  114.9 1.7 %fusion.6 = bf16[8,32,256]{2,1,0:T(8,128)(2,1)} fusion(f32[8,32,256]{2,1,0:T(8,128)S(1)} %collective-permute-done.2, f32[8,2,32,256]{3,2,1,0:T(8,128)} %copy-done.3), kind=kLoop, calls=%fused_computation.14 | loop fusion | flops 131072 | bytes 655360 | tf_op jit(solution)/shard_map/convert_element_type | solution.py:95
  116.5 10.6 %all-to-all-done.3 = bf16[64,8,256]{2,1,0:T(8,128)(2,1)S(1)} async-done(((bf16[64,8,256]{2,1,0:T(8,128)(2,1)}), bf16[64,8,256]{2,1,0:T(8,128)(2,1)S(1)}, u32[]{:S(2)}, u32[]{:S(2)}) %all-to-all-start.3) | async-done | bytes 262176 | tf_op jit(solution)/shard_map/all_to_all | solution.py:21
  127.2 4.2 %shard_map.101 = bf16[32,2,64,256]{3,2,1,0:T(8,128)(2,1)} custom-call(s32[2]{0:T(128)S(1)} %pad_add_fusion.core_ref, bf16[1,2048,512]{2,1,0:T(8,128)(2,1)S(1)} %bitcast.57, bf16[1,2048,512]{2,1,0:T(8,128)(2,1)} %bitcast.23.other_ref, bf16[512,256]{1,0:T(8,128)(2,1)S(1)} %bitcast.58), custom_call_target="tpu_custom_call" | custom-call | flops 1073741824 | bytes 6291456 | tf_op jit(solution)/shard_map/pallas_call | solution.py:38
  (37 shorter events, 6.2 us)
Async XLA Ops:
  7.2 60.3 %all-gather.2.cloned.1.call-start = ((), (), s32[]{:S(2)}) async-start(), calls=%async_computation.5 | async-start | bytes 2359296 | tf_op jit(solution)/shard_map/all_gather | solution.py:72
  30.6 6.6 %collective-permute-start = (bf16[32,2048]{1,0:T(8,128)(2,1)S(1)}, bf16[32,2048]{1,0:T(8,128)(2,1)S(1)}, u32[]{:S(2)}, u32[]{:S(2)}) collective-permute-start(bf16[32,2048]{1,0:T(8,128)(2,1)S(1)} %select_n.49), channel_id=1, source_target_pairs={{0,8},{8,0},{1,9},{9,1},{2,10},{10,2},{3,11},{11,3},{4,12},{12,4},... | collective-permute-start | bytes 393224 | tf_op jit(solution)/shard_map/ppermute | solution.py:68
  38.8 4.8 %copy-start.1 = (bf16[4096,256]{1,0:T(8,128)(2,1)S(1)}, bf16[4096,256]{1,0:T(8,128)(2,1)}, u32[]{:S(2)}) copy-start(bf16[4096,256]{1,0:T(8,128)(2,1)} %param.7) | copy-start | bytes 6291460
  38.8 31.0 %all-to-all-start.1 = ((bf16[8,2,32,2048]{3,2,1,0:T(8,128)(2,1)}), bf16[8,2,32,2048]{3,2,1,0:T(8,128)(2,1)}, u32[]{:S(2)}, u32[]{:S(2)}) async-start(bf16[8,2,32,2048]{3,2,1,0:T(8,128)(2,1)} %broadcast_in_dim.11), calls=%async_computation.1 | async-start | bytes 4194304 | tf_op jit(solution)/shard_map/all_to_all | solution.py:21
  43.5 0.9 copy-start.4
  43.5 68.0 %reduce-scatter.2.cloned.1.call-start = ((), (), s32[]{:S(2)}) async-start(), calls=%async_computation.6 | async-start | bytes 2621440 | tf_op jit(solution)/shard_map/reduce_scatter | solution.py:85
  44.4 4.7 %collective-permute-start.1 = (bf16[256,256]{1,0:T(8,128)(2,1)S(1)}, bf16[256,256]{1,0:T(8,128)(2,1)}, u32[]{:S(2)}, u32[]{:S(2)}) collective-permute-start(bf16[256,256]{1,0:T(8,128)(2,1)S(1)} %copy-done.4), channel_id=1, source_target_pairs={{0,8},{8,0},{1,9},{9,1},{2,10},{10,2},{3,11},{11,3},{4,12},{12,4},... | collective-permute-start | bytes 393224 | tf_op jit(solution)/shard_map/ppermute | solution.py:68
  67.5 2.4 %copy-start = (bf16[2048,512]{1,0:T(8,128)(2,1)S(1)}, bf16[2048,512]{1,0:T(8,128)(2,1)}, u32[]{:S(2)}) copy-start(bf16[2048,512]{1,0:T(8,128)(2,1)} %all-gather.2.cloned.1.call-done) | copy-start | bytes 6291460
  73.7 29.8 %all-to-all-start.2 = ((bf16[64,8,256]{2,1,0:T(8,128)(2,1)}), bf16[64,8,256]{2,1,0:T(8,128)(2,1)S(1)}, u32[]{:S(2)}, u32[]{:S(2)}) async-start(bf16[64,8,256]{2,1,0:T(8,128)(2,1)} %fusion.1), calls=%async_computation.2 | async-start | bytes 524288 | tf_op jit(solution)/shard_map/all_to_all | solution.py:91
  87.9 17.9 %copy-start.5 = (f32[8,256]{1,0:T(8,128)S(1)}, f32[8,256]{1,0:T(8,128)}, u32[]{:S(2)}) copy-start(f32[8,256]{1,0:T(8,128)} %param.11) | copy-start | bytes 24580
  87.9 17.9 %copy-start.6 = (f32[8,256]{1,0:T(8,128)S(1)}, f32[8,256]{1,0:T(8,128)}, u32[]{:S(2)}) copy-start(f32[8,256]{1,0:T(8,128)} %param.10) | copy-start | bytes 24580
  90.3 0.8 copy-start.3
  91.1 12.5 %collective-permute-start.2 = (f32[8,32,256]{2,1,0:T(8,128)S(1)}, f32[8,32,256]{2,1,0:T(8,128)S(1)}, u32[]{:S(2)}, u32[]{:S(2)}) collective-permute-start(f32[8,32,256]{2,1,0:T(8,128)S(1)} %slice_bitcast_fusion), channel_id=1, source_target_pairs={{0,8},{8,0},{1,9},{9,1},{2,10},{10,2},{3,11},{11,3},{4,12},{12,4},... | collective-permute-start | bytes 786440 | tf_op jit(solution)/shard_map/ppermute | solution.py:68
  103.6 23.6 %collective-permute-start.4 = (bf16[2048,512]{1,0:T(8,128)(2,1)S(1)}, bf16[2048,512]{1,0:T(8,128)(2,1)}, u32[]{:S(2)}, u32[]{:S(2)}) collective-permute-start(bf16[2048,512]{1,0:T(8,128)(2,1)S(1)} %copy-done), channel_id=1, source_target_pairs={{0,8},{8,0},{1,9},{9,1},{2,10},{10,2},{3,11},{11,3},{4,12},{12,4},... | collective-permute-start | bytes 6291464 | tf_op jit(solution)/shard_map/ppermute | solution.py:68
  107.2 20.0 %all-to-all-start.3 = ((bf16[64,8,256]{2,1,0:T(8,128)(2,1)}), bf16[64,8,256]{2,1,0:T(8,128)(2,1)S(1)}, u32[]{:S(2)}, u32[]{:S(2)}) async-start(bf16[64,8,256]{2,1,0:T(8,128)(2,1)} %broadcast_in_dim.28), calls=%async_computation.4 | async-start | bytes 524288 | tf_op jit(solution)/shard_map/all_to_all | solution.py:21
  112.5 18.9 %collective-permute-start.3 = (bf16[32,4096]{1,0:T(8,128)(2,1)S(1)}, bf16[32,4096]{1,0:T(8,128)(2,1)S(1)}, u32[]{:S(2)}, u32[]{:S(2)}) collective-permute-start(bf16[32,4096]{1,0:T(8,128)(2,1)S(1)} %dynamic-slice_bitcast_fusion), channel_id=1, source_target_pairs={{0,4},{4,0},{1,5},{5,1},{2,6},{6,2},{3,7},{7,3},{8,12},{12,8},{9,1... | collective-permute-start | bytes 786440 | tf_op jit(solution)/shard_map/ppermute | solution.py:106
  127.1 4.2 %copy-start.2 = (bf16[64,4096]{1,0:T(8,128)(2,1)S(1)}, bf16[64,4096]{1,0:T(8,128)(2,1)}, u32[]{:S(2)}) copy-start(bf16[64,4096]{1,0:T(8,128)(2,1)} %reduce-scatter.2.cloned.1.call-done) | copy-start | bytes 1572868
Sparse Core Ops, SparseCore 0:
  27.7 39.7 all-gather.1
  70.3 37.7 reduce-scatter.1

commit v5 on v3

--- a/solution.py
+++ b/solution.py
@@ -67,7 +67,7 @@
     def swap(value):
         return lax.ppermute(value, "c", SWAP)
 
-    proj_z = copies_to(proj, "zh", 4)
+    proj_z = lax.all_gather(proj, "zh", axis=0, tiled=False)
     x_seq, grad_out, moment1, proj_z = lax.optimization_barrier((x_seq, grad_out, moment1, proj_z))
     proj_own = lax.all_gather(proj_z.reshape(4 * rows, rank), "y", axis=0, tiled=True)
 

time: 140 us -> 140 us (level)
    all_gather x0 -> x1, blocking collectives: none -> 19.7 us  [per_device(): proj_z = lax.all_gather(proj, 'zh', axis=0, tiled=False)]
    all_to_all x1 -> x0, blocking collectives: 19.5 us -> none  [copies_to(): return lax.all_to_all(copies, axes, 0, 0, tiled=True)]
    all_gather x1, waiting for transfers between devices: 15.1 us -> 16.6 us  [per_device(): lax.all_gather(proj_z.reshape(4 * rows, rank), 'y', axis=0, tiled=True)]
    broadcast_in_dim x3 -> x2, local copies, waits for them, and re-layouts: 3.16 us -> 2.3 us  [copies_to(): copies = jnp.broadcast_to(value[None], (count, *value.shape))]
where the time goes in v5:
time: 140 us; the launch traced here: 138 us
  starting transfers between devices  50.4 us (36%)
  waiting for transfers between devices  28.3 us (20%)
  blocking collectives  19.7 us (14%)
  between operations  14.3 us (10%)
  matrix products  8.24 us (6%)
  local copies, waits for them, and re-layouts  7.53 us (5%)
  other arithmetic  5.53 us (4%)
  Pallas kernels  4.22 us (3%)
    ppermute x6, starting transfers between devices, swap(): return lax.ppermute(value, 'c', SWAP)  24.6 us
    all_gather x1, blocking collectives, per_device(): proj_z = lax.all_gather(proj, 'zh', axis=0, tiled=False)  19.7 us
    all_gather x1, waiting for transfers between devices, per_device(): lax.all_gather(proj_z.reshape(4 * rows, rank), 'y', axis=0, tiled=True)  16.6 us
    all_to_all x2, starting transfers between devices, copies_to(): return lax.all_to_all(copies, axes, 0, 0, tiled=True)  13.1 us
    all_to_all x1, starting transfers between devices, per_device(): lax.all_to_all(local, RING, 0, 0, tiled=True).astype(f32)  10.2 us
    all_to_all x2, waiting for transfers between devices, copies_to(): return lax.all_to_all(copies, axes, 0, 0, tiled=True)  9.53 us
    pallas_call x1, Pallas kernels, update_rows(): pl.pallas_call(kernel, out_shape=jax.ShapeDtypeStruct((half // rows, 2, r...  4.22 us
    dot_general x1, matrix products, per_device(): jnp.dot(both_x, proj_own, preferred_element_type=f32).astype(bf16)  2.83 us
  transfers between devices with their start and end apart: 12, of which 5 were waited for; matrix products, arithmetic and copies ran while one was open for 14% of the time, Pallas kernels for 3%

profile of v5, /device:TPU:1, one launch (start us, length us, event | category | flops | bytes accessed | tf_op | source)
XLA Modules:
  0.0 138.1 jit_solution(9913458136194115429)
XLA Ops:
  7.2 19.7 %all-gather = bf16[256,512]{1,0:T(8,128)(2,1)} all-gather(bf16[64,512]{1,0:T(8,128)(2,1)} %param.9), channel_id=2, replica_groups=mesh['y'=8,'zh'=4,'c'=2,'zl'=2,'x'=4] {'zh'}, dimensions={0}, use_global_device_ids=true | all-gather | bytes 327680 | tf_op jit(solution)/shard_map/all_gather | solution.py:70
  26.9 1.5 %reshape.89 = bf16[32,32,2,64]{3,2,1,0:T(2,128)(2,1)S(1)} reshape(bf16[32,4096]{1,0:T(8,128)(2,1)} %param.6) | data formatting | bytes 524288 | tf_op jit(solution)/shard_map/reshape | solution.py:74
  28.4 1.2 fusion.8
  29.9 5.5 %collective-permute-start = (bf16[32,2048]{1,0:T(8,128)(2,1)S(1)}, bf16[32,2048]{1,0:T(8,128)(2,1)S(1)}, u32[]{:S(2)}, u32[]{:S(2)}) collective-permute-start(bf16[32,2048]{1,0:T(8,128)(2,1)S(1)} %select_n.73), channel_id=1, source_target_pairs={{0,8},{8,0},{1,9},{9,1},{2,10},{10,2},{3,11},{11,3},{4,12},{12,4},... | collective-permute-start | bytes 393224 | tf_op jit(solution)/shard_map/ppermute | solution.py:68
  36.5 1.6 %broadcast_in_dim.8 = bf16[8,2,32,2048]{3,2,1,0:T(8,128)(2,1)} broadcast(bf16[2,32,2048]{2,1,0:T(8,128)(2,1)S(1)} %pad_maximum_fusion), dimensions={1,2,3} | broadcast | bytes 2359296 | tf_op jit(solution)/shard_map/broadcast_in_dim | solution.py:20
  38.0 5.3 %all-to-all-start = ((bf16[8,2,32,2048]{3,2,1,0:T(8,128)(2,1)}), bf16[8,2,32,2048]{3,2,1,0:T(8,128)(2,1)}, u32[]{:S(2)}, u32[]{:S(2)}) async-start(bf16[8,2,32,2048]{3,2,1,0:T(8,128)(2,1)} %broadcast_in_dim.8), calls=%async_computation | async-start | bytes 4194304 | tf_op jit(solution)/shard_map/all_to_all | solution.py:21
  43.4 2.6 %collective-permute-start.2 = (f32[2,8,256]{2,1,0:T(8,128)S(1)}, f32[2,8,256]{2,1,0:T(8,128)S(1)}, u32[]{:S(2)}, u32[]{:S(2)}) collective-permute-start(f32[2,8,256]{2,1,0:T(8,128)S(1)} %pad_maximum_fusion.3), channel_id=1, source_target_pairs={{0,8},{8,0},{1,9},{9,1},{2,10},{10,2},{3,11},{11,3},{4,12},{12,4},... | collective-permute-start | bytes 49160 | tf_op jit(solution)/shard_map/ppermute | solution.py:68
  46.0 1.9 %collective-permute-start.1 = (bf16[256,256]{1,0:T(8,128)(2,1)S(1)}, bf16[256,256]{1,0:T(8,128)(2,1)}, u32[]{:S(2)}, u32[]{:S(2)}) collective-permute-start(bf16[256,256]{1,0:T(8,128)(2,1)S(1)} %copy-done.4), channel_id=1, source_target_pairs={{0,8},{8,0},{1,9},{9,1},{2,10},{10,2},{3,11},{11,3},{4,12},{12,4},... | collective-permute-start | bytes 393224 | tf_op jit(solution)/shard_map/ppermute | solution.py:68
  47.9 2.1 %convolution_convert_fusion = bf16[256,4096]{1,0:T(8,128)(2,1)} fusion(bf16[256,256]{1,0:T(8,128)(2,1)S(1)} %bitcast.76, bf16[4096,256]{1,0:T(8,128)(2,1)S(1)} %copy-done.1), kind=kOutput, calls=%fused_computation | convolution fusion | flops 537919488 | bytes 4325376 | tf_op jit(solution)/shard_map/dot_general | solution.py:79
  51.6 16.6 %all-gather.3.cloned.1.call-done = bf16[2048,512]{1,0:T(8,128)(2,1)} async-done(((bf16[256,512]{1,0:T(8,128)(2,1)}), bf16[2048,512]{1,0:T(8,128)(2,1)}) %all-gather.3.cloned.1.call-update) | async-done | bytes 2097168 | tf_op jit(solution)/shard_map/all_gather | solution.py:72
  68.3 1.3 all-to-all-done
  69.9 2.8 %convolution_convert_fusion.1 = bf16[512,512]{1,0:T(8,128)(2,1)S(1)} fusion(bf16[512,2048]{1,0:T(8,128)(2,1)} %bitcast.19, bf16[2048,512]{1,0:T(8,128)(2,1)S(1)} %copy-done), kind=kOutput, calls=%fused_computation.1 | convolution fusion | flops 1074003968 | bytes 4718592 | tf_op jit(solution)/shard_map/dot_general | solution.py:91
  72.7 1.1 fusion
  73.7 10.2 %all-to-all-start.1 = ((bf16[32,16,256]{2,1,0:T(8,128)(2,1)}), bf16[32,16,256]{2,1,0:T(8,128)(2,1)S(1)}, u32[]{:S(2)}, u32[]{:S(2)}) async-start(bf16[32,16,256]{2,1,0:T(8,128)(2,1)} %bitcast.81), calls=%async_computation.1 | async-start | bytes 524288 | tf_op jit(solution)/shard_map/all_to_all | solution.py:95
  84.0 6.5 %collective-permute-start.6 = (bf16[2048,512]{1,0:T(8,128)(2,1)S(1)}, bf16[2048,512]{1,0:T(8,128)(2,1)}, u32[]{:S(2)}, u32[]{:S(2)}) collective-permute-start(bf16[2048,512]{1,0:T(8,128)(2,1)S(1)} %copy-done), channel_id=1, source_target_pairs={{0,8},{8,0},{1,9},{9,1},{2,10},{10,2},{3,11},{11,3},{4,12},{12,4},... | collective-permute-start | bytes 6291464 | tf_op jit(solution)/shard_map/ppermute | solution.py:68
  90.5 2.3 %fusion.1 = f32[8,2,32,256]{3,2,1,0:T(8,128)S(1)} fusion(bf16[8,2,32,2048]{3,2,1,0:T(8,128)(2,1)} %all-to-all-done, bf16[2048,256]{1,0:T(8,128)(2,1)S(1)} %bitcast.75), kind=kOutput, calls=%fused_computation.5 | convolution fusion | flops 536870912 | bytes 3670016 | tf_op jit(solution)/shard_map/dot_general | solution.py:96
  93.6 1.9 %collective-permute-start.3 = (f32[8,32,256]{2,1,0:T(8,128)S(1)}, f32[8,32,256]{2,1,0:T(8,128)S(1)}, u32[]{:S(2)}, u32[]{:S(2)}) collective-permute-start(f32[8,32,256]{2,1,0:T(8,128)S(1)} %slice_bitcast_fusion), channel_id=1, source_target_pairs={{0,8},{8,0},{1,9},{9,1},{2,10},{10,2},{3,11},{11,3},{4,12},{12,4},... | collective-permute-start | bytes 786440 | tf_op jit(solution)/shard_map/ppermute | solution.py:68
  95.7 1.4 collective-permute-done.3
  97.0 6.2 %collective-permute-start.4 = (f32[16,256]{1,0:T(8,128)S(1)}, f32[16,256]{1,0:T(8,128)S(1)}, u32[]{:S(2)}, u32[]{:S(2)}) collective-permute-start(f32[16,256]{1,0:T(8,128)S(1)} %convert_reduce_fusion), channel_id=1, source_target_pairs={{0,8},{8,0},{1,9},{9,1},{2,10},{10,2},{3,11},{11,3},{4,12},{12,4},... | collective-permute-start | bytes 49160 | tf_op jit(solution)/shard_map/ppermute | solution.py:68
  103.3 1.7 %fusion.5 = bf16[8,32,256]{2,1,0:T(8,128)(2,1)} fusion(f32[8,32,256]{2,1,0:T(8,128)S(1)} %collective-permute-done.3, f32[8,2,32,256]{3,2,1,0:T(8,128)} %copy-done.3), kind=kLoop, calls=%fused_computation.13 | loop fusion | flops 131072 | bytes 655360 | tf_op jit(solution)/shard_map/convert_element_type | solution.py:98
  105.7 7.8 %all-to-all-start.2 = ((bf16[32,16,256]{2,1,0:T(8,128)(2,1)}), bf16[32,16,256]{2,1,0:T(8,128)(2,1)S(1)}, u32[]{:S(2)}, u32[]{:S(2)}) async-start(bf16[32,16,256]{2,1,0:T(8,128)(2,1)} %broadcast_in_dim.21), calls=%async_computation.3 | async-start | bytes 524288 | tf_op jit(solution)/shard_map/all_to_all | solution.py:21
  115.1 2.4 %collective-permute-start.5 = (bf16[32,4096]{1,0:T(8,128)(2,1)S(1)}, bf16[32,4096]{1,0:T(8,128)(2,1)S(1)}, u32[]{:S(2)}, u32[]{:S(2)}) collective-permute-start(bf16[32,4096]{1,0:T(8,128)(2,1)S(1)} %dynamic-slice_bitcast_fusion), channel_id=1, source_target_pairs={{0,4},{4,0},{1,5},{5,1},{2,6},{6,2},{3,7},{7,3},{8,12},{12,8},{9,1... | collective-permute-start | bytes 786440 | tf_op jit(solution)/shard_map/ppermute | solution.py:111
  118.1 8.2 %all-to-all-done.2 = bf16[32,16,256]{2,1,0:T(8,128)(2,1)S(1)} async-done(((bf16[32,16,256]{2,1,0:T(8,128)(2,1)}), bf16[32,16,256]{2,1,0:T(8,128)(2,1)S(1)}, u32[]{:S(2)}, u32[]{:S(2)}) %all-to-all-start.2) | async-done | bytes 262176 | tf_op jit(solution)/shard_map/all_to_all | solution.py:21
  126.3 4.2 %shard_map.101 = bf16[32,2,64,256]{3,2,1,0:T(8,128)(2,1)} custom-call(s32[2]{0:T(128)S(1)} %pad_add_fusion.core_ref, bf16[1,2048,512]{2,1,0:T(8,128)(2,1)S(1)} %bitcast.71, bf16[1,2048,512]{2,1,0:T(8,128)(2,1)} %bitcast.30.other_ref, bf16[512,256]{1,0:T(8,128)(2,1)S(1)} %bitcast.72), custom_call_target="tpu_custom_call" | custom-call | flops 1073741824 | bytes 6291456 | tf_op jit(solution)/shard_map/pallas_call | solution.py:38
  (47 shorter events, 8.0 us)
Async XLA Ops:
  7.2 61.1 %all-gather.3.cloned.1.call-start = ((), (), s32[]{:S(2)}) async-start(), calls=%async_computation.4 | async-start | bytes 2359296 | tf_op jit(solution)/shard_map/all_gather | solution.py:72
  29.9 6.5 %collective-permute-start = (bf16[32,2048]{1,0:T(8,128)(2,1)S(1)}, bf16[32,2048]{1,0:T(8,128)(2,1)S(1)}, u32[]{:S(2)}, u32[]{:S(2)}) collective-permute-start(bf16[32,2048]{1,0:T(8,128)(2,1)S(1)} %select_n.73), channel_id=1, source_target_pairs={{0,8},{8,0},{1,9},{9,1},{2,10},{10,2},{3,11},{11,3},{4,12},{12,4},... | collective-permute-start | bytes 393224 | tf_op jit(solution)/shard_map/ppermute | solution.py:68
  38.0 5.3 %copy-start.6 = (f32[8,256]{1,0:T(8,128)S(1)}, f32[8,256]{1,0:T(8,128)}, u32[]{:S(2)}) copy-start(f32[8,256]{1,0:T(8,128)} %param.11) | copy-start | bytes 24580
  38.0 5.3 %copy-start.7 = (f32[8,256]{1,0:T(8,128)S(1)}, f32[8,256]{1,0:T(8,128)}, u32[]{:S(2)}) copy-start(f32[8,256]{1,0:T(8,128)} %param.10) | copy-start | bytes 24580
  38.0 7.9 %copy-start.4 = (bf16[256,256]{1,0:T(8,128)(2,1)S(1)}, bf16[256,256]{1,0:T(8,128)(2,1)}, u32[]{:S(2)}) copy-start(bf16[256,256]{1,0:T(8,128)(2,1)} %param.8) | copy-start | bytes 393220
  38.0 9.9 %copy-start.1 = (bf16[4096,256]{1,0:T(8,128)(2,1)S(1)}, bf16[4096,256]{1,0:T(8,128)(2,1)}, u32[]{:S(2)}) copy-start(bf16[4096,256]{1,0:T(8,128)(2,1)} %param.7) | copy-start | bytes 6291460
  38.0 31.6 %all-to-all-start = ((bf16[8,2,32,2048]{3,2,1,0:T(8,128)(2,1)}), bf16[8,2,32,2048]{3,2,1,0:T(8,128)(2,1)}, u32[]{:S(2)}, u32[]{:S(2)}) async-start(bf16[8,2,32,2048]{3,2,1,0:T(8,128)(2,1)} %broadcast_in_dim.8), calls=%async_computation | async-start | bytes 4194304 | tf_op jit(solution)/shard_map/all_to_all | solution.py:21
  43.3 70.8 %reduce-scatter.2.cloned.1.call-start = ((), (), s32[]{:S(2)}) async-start(), calls=%async_computation.5 | async-start | bytes 2621440 | tf_op jit(solution)/shard_map/reduce_scatter | solution.py:89
  43.4 6.7 %collective-permute-start.2 = (f32[2,8,256]{2,1,0:T(8,128)S(1)}, f32[2,8,256]{2,1,0:T(8,128)S(1)}, u32[]{:S(2)}, u32[]{:S(2)}) collective-permute-start(f32[2,8,256]{2,1,0:T(8,128)S(1)} %pad_maximum_fusion.3), channel_id=1, source_target_pairs={{0,8},{8,0},{1,9},{9,1},{2,10},{10,2},{3,11},{11,3},{4,12},{12,4},... | collective-permute-start | bytes 49160 | tf_op jit(solution)/shard_map/ppermute | solution.py:68
  46.0 4.8 %collective-permute-start.1 = (bf16[256,256]{1,0:T(8,128)(2,1)S(1)}, bf16[256,256]{1,0:T(8,128)(2,1)}, u32[]{:S(2)}, u32[]{:S(2)}) collective-permute-start(bf16[256,256]{1,0:T(8,128)(2,1)S(1)} %copy-done.4), channel_id=1, source_target_pairs={{0,8},{8,0},{1,9},{9,1},{2,10},{10,2},{3,11},{11,3},{4,12},{12,4},... | collective-permute-start | bytes 393224 | tf_op jit(solution)/shard_map/ppermute | solution.py:68
  68.3 1.6 %copy-start = (bf16[2048,512]{1,0:T(8,128)(2,1)S(1)}, bf16[2048,512]{1,0:T(8,128)(2,1)}, u32[]{:S(2)}) copy-start(bf16[2048,512]{1,0:T(8,128)(2,1)} %all-gather.3.cloned.1.call-done) | copy-start | bytes 6291460
  73.7 21.9 %all-to-all-start.1 = ((bf16[32,16,256]{2,1,0:T(8,128)(2,1)}), bf16[32,16,256]{2,1,0:T(8,128)(2,1)S(1)}, u32[]{:S(2)}, u32[]{:S(2)}) async-start(bf16[32,16,256]{2,1,0:T(8,128)(2,1)} %bitcast.81), calls=%async_computation.1 | async-start | bytes 524288 | tf_op jit(solution)/shard_map/all_to_all | solution.py:95
  84.0 21.0 %copy-start.5 = (f32[2,16,256]{2,1,0:T(8,128)S(1)}, f32[2,16,256]{2,1,0:T(8,128)}, u32[]{:S(2)}) copy-start(f32[2,16,256]{2,1,0:T(8,128)} %copy_bitcast_fusion) | copy-start | bytes 98308
  84.0 42.3 %collective-permute-start.6 = (bf16[2048,512]{1,0:T(8,128)(2,1)S(1)}, bf16[2048,512]{1,0:T(8,128)(2,1)}, u32[]{:S(2)}, u32[]{:S(2)}) collective-permute-start(bf16[2048,512]{1,0:T(8,128)(2,1)S(1)} %copy-done), channel_id=1, source_target_pairs={{0,8},{8,0},{1,9},{9,1},{2,10},{10,2},{3,11},{11,3},{4,12},{12,4},... | collective-permute-start | bytes 6291464 | tf_op jit(solution)/shard_map/ppermute | solution.py:68
  92.8 0.8 copy-start.3
  93.6 3.4 %collective-permute-start.3 = (f32[8,32,256]{2,1,0:T(8,128)S(1)}, f32[8,32,256]{2,1,0:T(8,128)S(1)}, u32[]{:S(2)}, u32[]{:S(2)}) collective-permute-start(f32[8,32,256]{2,1,0:T(8,128)S(1)} %slice_bitcast_fusion), channel_id=1, source_target_pairs={{0,8},{8,0},{1,9},{9,1},{2,10},{10,2},{3,11},{11,3},{4,12},{12,4},... | collective-permute-start | bytes 786440 | tf_op jit(solution)/shard_map/ppermute | solution.py:68
  97.0 7.9 %collective-permute-start.4 = (f32[16,256]{1,0:T(8,128)S(1)}, f32[16,256]{1,0:T(8,128)S(1)}, u32[]{:S(2)}, u32[]{:S(2)}) collective-permute-start(f32[16,256]{1,0:T(8,128)S(1)} %convert_reduce_fusion), channel_id=1, source_target_pairs={{0,8},{8,0},{1,9},{9,1},{2,10},{10,2},{3,11},{11,3},{4,12},{12,4},... | collective-permute-start | bytes 49160 | tf_op jit(solution)/shard_map/ppermute | solution.py:68
  105.7 20.6 %all-to-all-start.2 = ((bf16[32,16,256]{2,1,0:T(8,128)(2,1)}), bf16[32,16,256]{2,1,0:T(8,128)(2,1)S(1)}, u32[]{:S(2)}, u32[]{:S(2)}) async-start(bf16[32,16,256]{2,1,0:T(8,128)(2,1)} %broadcast_in_dim.21), calls=%async_computation.3 | async-start | bytes 524288 | tf_op jit(solution)/shard_map/all_to_all | solution.py:21
  115.1 15.4 %collective-permute-start.5 = (bf16[32,4096]{1,0:T(8,128)(2,1)S(1)}, bf16[32,4096]{1,0:T(8,128)(2,1)S(1)}, u32[]{:S(2)}, u32[]{:S(2)}) collective-permute-start(bf16[32,4096]{1,0:T(8,128)(2,1)S(1)} %dynamic-slice_bitcast_fusion), channel_id=1, source_target_pairs={{0,4},{4,0},{1,5},{5,1},{2,6},{6,2},{3,7},{7,3},{8,12},{12,8},{9,1... | collective-permute-start | bytes 786440 | tf_op jit(solution)/shard_map/ppermute | solution.py:111
  126.3 4.2 %copy-start.2 = (bf16[64,4096]{1,0:T(8,128)(2,1)S(1)}, bf16[64,4096]{1,0:T(8,128)(2,1)}, u32[]{:S(2)}) copy-start(bf16[64,4096]{1,0:T(8,128)(2,1)} %reduce-scatter.2.cloned.1.call-done) | copy-start | bytes 1572868
Sparse Core Ops, SparseCore 0:
  27.0 41.1 all-gather.2
  71.1 37.7 reduce-scatter.1
